TPU v7x, 32 devices: a whole 2x2x4 slice. The times are simulated.
32 devices in a mesh: rows: 8 (over z, y), heads: 4 (over x, core).
Axes of the slice: x: 2, y: 2, z: 4, core: 2. Of those that a mesh axis runs over, the one named last changes fastest.
Arguments:
- tokens: bfloat16 [8, 2048, 768], P('rows', 'heads'), may hold values from -6 to 6
- lengths: int32 [8], P('rows'), may hold values from 8 to 2048, as said below
- w_qkv: bfloat16 [3, 768, 768], P(None, None, 'heads'), may hold values from -0.21875 to 0.21875
- w_out: bfloat16 [768, 768], P('heads'), may hold values from -1.25 to 1.25
- w_gate: bfloat16 [768, 3072], P(None, 'heads'), may hold values from -0.21875 to 0.21875
- w_up: bfloat16 [768, 3072], P(None, 'heads'), may hold values from -0.21875 to 0.21875
- w_down: bfloat16 [3072, 768], P('heads'), may hold values from -0.109375 to 0.109375
- gain_attn: float32 [768], replicated, may hold values from 0.25 to 1.75
- gain_mlp: float32 [768], replicated, may hold values from 0.25 to 1.75
- cotangent: bfloat16 [8, 2048, 768], P('rows', 'heads'), may hold values from -12 to 12
Outputs:
- layer_out: bfloat16 [8, 2048, 768], P('rows', 'heads')
- input_grad: bfloat16 [8, 2048, 768], P('rows', 'heads')
- grad_qkv: float32 [3, 768, 768], P(None, None, 'heads')
- grad_out: float32 [768, 768], P('heads')
- grad_gate: float32 [768, 3072], P(None, 'heads')
- grad_up: float32 [768, 3072], P(None, 'heads')
- grad_down: float32 [3072, 768], P('heads')
- grad_gain_attn: float32 [768], replicated
- grad_gain_mlp: float32 [768], replicated
Inputs may be any that keep to these rules, and one draw needn't show every extreme that they name: `lengths`: in each aligned block of 1 row one row, chosen from the seed, has more than 1536 live tokens; at least one row has all 2048 positions live; the other rows are short ones of at most 64 tokens or longer ones of 64 or more.
All inputs are finite; a program needn't handle non-finite values.
Results may differ from a plain program's by a relative error of at most 0.02.
Values may be sent and summed in bfloat16 or wider, within the bound.
A program may use at most 128 MiB of HBM per device.

v0:
```python
import jax
import jax.numpy as jnp
from jax import lax
from jax.sharding import PartitionSpec as P

HEAD = 64


eps = 1e-05
rope_base = 1000.0


def rotary_tables(length):
    half = HEAD // 2
    freqs = rope_base ** (-jnp.arange(half).astype(jnp.float32) / half)
    angles = jnp.arange(length).astype(jnp.float32)[:, None] * freqs[None, :]
    return (jnp.cos(angles), jnp.sin(angles))


def rotate(u, cosine, sine, sign):
    half = HEAD // 2
    first = u[..., :half]
    second = u[..., half:]
    cosine = cosine[None, :, None, :]
    sine = sine[None, :, None, :]
    return jnp.concatenate(
        [first * cosine - sign * second * sine, second * cosine + sign * first * sine], axis=-1
    )


def normalize(resid):
    centre = resid - jnp.mean(resid, axis=-1, keepdims=True)
    inverse = lax.rsqrt(jnp.mean(centre * centre, axis=-1, keepdims=True) + eps)
    return (centre * inverse, inverse)


def norm_back(grad_norm, normed, inverse):
    first = jnp.mean(grad_norm, axis=-1, keepdims=True)
    second = jnp.mean(grad_norm * normed, axis=-1, keepdims=True)
    return inverse * (grad_norm - first - normed * second)


def block_scores(q_block, keys, valid):
    scores = jnp.einsum("qhd,khd->hqk", q_block, keys, preferred_element_type=jnp.float32) * 0.125
    return jnp.where(valid[None, None, :], scores, -1e30)


def attend_row(q_row, k_row, v_row, valid):
    length, heads_here, size = q_row.shape
    block = min(512, length)
    q_blocks = q_row.reshape(length // block, block, heads_here, size)
    values_wide = v_row.astype(jnp.float32)

    def one_block(q_block):
        scores = block_scores(q_block, k_row, valid)
        top = jnp.max(scores, axis=2, keepdims=True)
        expo = jnp.exp(scores - top)
        total = jnp.sum(expo, axis=2, keepdims=True)
        probs = expo / total
        result = jnp.einsum("hqk,khd->qhd", probs, values_wide, precision=lax.Precision.HIGHEST)
        return (result, (top + jnp.log(total))[:, :, 0])

    results, lse = lax.map(one_block, q_blocks)
    return (results.reshape(length, heads_here, size), lse)


def attend_back(q_row, k_row, v_row, o_row, lse_row, do_row, valid):
    length, heads_here, size = q_row.shape
    block = min(512, length)
    count = length // block
    q_blocks = q_row.reshape(count, block, heads_here, size)
    o_blocks = o_row.reshape(count, block, heads_here, size)
    do_blocks = do_row.reshape(count, block, heads_here, size)

    def step(carry, item):
        grad_keys, grad_values = carry
        q_block, o_block, do_block, lse_block = item
        scores = block_scores(q_block, k_row, valid)
        probs = jnp.exp(scores - lse_block[:, :, None])
        do_wide = do_block.astype(jnp.float32)
        grad_probs = jnp.einsum("qhd,khd->hqk", do_block, v_row, preferred_element_type=jnp.float32)
        delta = jnp.sum(do_wide * o_block, axis=2).T
        grad_scores = (probs * (grad_probs - delta[:, :, None]) * 0.125).astype(jnp.bfloat16)
        grad_query = jnp.einsum(
            "hqk,khd->qhd", grad_scores, k_row, preferred_element_type=jnp.float32
        )
        grad_keys = grad_keys + jnp.einsum(
            "hqk,qhd->khd", grad_scores, q_block, preferred_element_type=jnp.float32
        )
        grad_values = grad_values + jnp.einsum(
            "hqk,qhd->khd", probs, do_wide, precision=lax.Precision.HIGHEST
        )
        return ((grad_keys, grad_values), grad_query)

    start = (
        jnp.zeros((length, heads_here, size), jnp.float32),
        jnp.zeros((length, heads_here, size), jnp.float32),
    )
    (grad_keys, grad_values), grad_query = lax.scan(
        step, start, (q_blocks, o_blocks, do_blocks, lse_row)
    )
    return (grad_query.reshape(length, heads_here, size), grad_keys, grad_values)


def on_device(tokens, lengths, w_qkv, w_out, w_gate, w_up, w_down, gain_attn, gain_mlp, cotangent):
    whole = lax.all_gather(tokens, "heads", axis=1, tiled=True)
    seq_rows, length, width = whole.shape
    heads_here = w_qkv.shape[2] // HEAD
    cosine, sine = rotary_tables(length)
    valid_all = jnp.arange(length)[None, :] < lengths[:, None]
    projected = jnp.einsum("rld,cde->crle", whole, w_qkv, preferred_element_type=jnp.float32)
    projected = projected.reshape(3, seq_rows, length, heads_here, HEAD)
    query = rotate(projected[0], cosine, sine, 1.0).astype(jnp.bfloat16)
    keys = rotate(projected[1], cosine, sine, 1.0).astype(jnp.bfloat16)
    values = projected[2].astype(jnp.bfloat16)

    def attend_one(item):
        return attend_row(item[0], item[1], item[2], item[3])

    attended, lse_all = lax.map(attend_one, (query, keys, values, valid_all))
    attended_low = attended.astype(jnp.bfloat16).reshape(seq_rows, length, heads_here * HEAD)
    attn_terms = jnp.einsum("rle,ed->rld", attended_low, w_out, preferred_element_type=jnp.float32)
    attn_sum = lax.psum_scatter(
        attn_terms.astype(jnp.bfloat16), "heads", scatter_dimension=1, tiled=True
    ).astype(jnp.float32)
    norm_one, inverse_one = normalize(tokens.astype(jnp.float32) + attn_sum)
    normed_one = norm_one * gain_attn
    normed_whole = lax.all_gather(normed_one.astype(jnp.bfloat16), "heads", axis=1, tiled=True)
    gate = jnp.einsum("rld,df->rlf", normed_whole, w_gate, preferred_element_type=jnp.float32)
    upper = jnp.einsum("rld,df->rlf", normed_whole, w_up, preferred_element_type=jnp.float32)
    activated = jax.nn.silu(gate)
    hidden = (activated * upper).astype(jnp.bfloat16)
    mlp_terms = jnp.einsum("rlf,fd->rld", hidden, w_down, preferred_element_type=jnp.float32)
    mlp_sum = lax.psum_scatter(
        mlp_terms.astype(jnp.bfloat16), "heads", scatter_dimension=1, tiled=True
    ).astype(jnp.float32)
    norm_two, inverse_two = normalize(normed_one + mlp_sum)
    layer_out = (norm_two * gain_mlp).astype(jnp.bfloat16)
    grad_output = cotangent.astype(jnp.float32)
    grad_gain_mlp = jnp.sum(grad_output * norm_two, axis=(0, 1))
    grad_resid_two = norm_back(grad_output * gain_mlp, norm_two, inverse_two)
    grad_mlp_whole = lax.all_gather(
        grad_resid_two.astype(jnp.bfloat16), "heads", axis=1, tiled=True
    )
    grad_hidden = jnp.einsum(
        "rld,fd->rlf", grad_mlp_whole, w_down, preferred_element_type=jnp.float32
    )
    grad_down = jnp.einsum(
        "rlf,rld->fd", hidden, grad_mlp_whole, preferred_element_type=jnp.float32
    )
    sigmoid_gate = jax.nn.sigmoid(gate)
    grad_gate_act = (
        grad_hidden * upper * sigmoid_gate * (1.0 + gate * (1.0 - sigmoid_gate))
    ).astype(jnp.bfloat16)
    grad_up_act = (grad_hidden * activated).astype(jnp.bfloat16)
    grad_gate = jnp.einsum(
        "rld,rlf->df", normed_whole, grad_gate_act, preferred_element_type=jnp.float32
    )
    grad_up = jnp.einsum(
        "rld,rlf->df", normed_whole, grad_up_act, preferred_element_type=jnp.float32
    )
    normed_terms = jnp.einsum(
        "rlf,df->rld", grad_gate_act, w_gate, preferred_element_type=jnp.float32
    )
    normed_terms = normed_terms + jnp.einsum(
        "rlf,df->rld", grad_up_act, w_up, preferred_element_type=jnp.float32
    )
    grad_normed = grad_resid_two + lax.psum_scatter(
        normed_terms.astype(jnp.bfloat16), "heads", scatter_dimension=1, tiled=True
    ).astype(jnp.float32)
    grad_gain_attn = jnp.sum(grad_normed * norm_one, axis=(0, 1))
    grad_resid_one = norm_back(grad_normed * gain_attn, norm_one, inverse_one)
    grad_attn_whole = lax.all_gather(
        grad_resid_one.astype(jnp.bfloat16), "heads", axis=1, tiled=True
    )
    grad_attended = jnp.einsum(
        "rld,ed->rle", grad_attn_whole, w_out, preferred_element_type=jnp.float32
    )
    grad_attended = grad_attended.astype(jnp.bfloat16).reshape(seq_rows, length, heads_here, HEAD)
    grad_out = jnp.einsum(
        "rle,rld->ed", attended_low, grad_attn_whole, preferred_element_type=jnp.float32
    )

    def back_one(item):
        return attend_back(item[0], item[1], item[2], item[3], item[4], item[5], item[6])

    grad_query, grad_keys, grad_values = lax.map(
        back_one, (query, keys, values, attended, lse_all, grad_attended, valid_all)
    )
    grad_query = rotate(grad_query, cosine, sine, -1.0).astype(jnp.bfloat16)
    grad_keys = rotate(grad_keys, cosine, sine, -1.0).astype(jnp.bfloat16)
    grad_values = grad_values.astype(jnp.bfloat16)
    grad_proj = jnp.stack([grad_query, grad_keys, grad_values]).reshape(
        3, seq_rows, length, heads_here * HEAD
    )
    grad_qkv = jnp.einsum("rld,crle->cde", whole, grad_proj, preferred_element_type=jnp.float32)
    input_terms = jnp.einsum("crle,cde->rld", grad_proj, w_qkv, preferred_element_type=jnp.float32)
    input_grad = (
        grad_resid_one
        + lax.psum_scatter(
            input_terms.astype(jnp.bfloat16), "heads", scatter_dimension=1, tiled=True
        ).astype(jnp.float32)
    ).astype(jnp.bfloat16)
    grad_qkv, grad_out, grad_gate, grad_up, grad_down = lax.psum(
        (grad_qkv, grad_out, grad_gate, grad_up, grad_down), "rows"
    )
    grad_gain_attn, grad_gain_mlp = lax.psum((grad_gain_attn, grad_gain_mlp), ("rows", "heads"))
    return (
        layer_out,
        input_grad,
        grad_qkv,
        grad_out,
        grad_gate,
        grad_up,
        grad_down,
        grad_gain_attn,
        grad_gain_mlp,
    )


def solution(mesh):
    in_specs = (
        P("rows", "heads", None),
        P("rows"),
        P(None, None, "heads"),
        P("heads", None),
        P(None, "heads"),
        P(None, "heads"),
        P("heads", None),
        P(),
        P(),
        P("rows", "heads", None),
    )
    out_specs = (
        P("rows", "heads", None),
        P("rows", "heads", None),
        P(None, None, "heads"),
        P("heads", None),
        P(None, "heads"),
        P(None, "heads"),
        P("heads", None),
        P(),
        P(),
    )
    return jax.shard_map(
        on_device, mesh=mesh, in_specs=in_specs, out_specs=out_specs, check_vma=False
    )
```

profile of v0, /device:TPU:0, one launch (start us, length us, event | category | flops | bytes accessed | tf_op | source)
XLA Modules:
  0.0 898.8 jit_solution(16518853787004455013)
XLA Ops:
  9.8 31.0 %all-gather.5.cloned.1.call-done = bf16[1,2048,768]{2,1,0:T(8,128)(2,1)} async-done(((bf16[1,512,768]{2,1,0:T(8,128)(2,1)}), bf16[1,2048,768]{2,1,0:T(8,128)(2,1)}) %all-gather.5.cloned.1.call-update) | async-done | bytes 3145744 | tf_op jit(solution)/shard_map/all_gather | solution.py:106
  40.8 4.2 convolution_bitcast_fusion.2
  53.1 87.8 %while.48 = (s32[]{:T(128)}, f32[4,512,3,64]{1,3,2,0:T(8,128)}, f32[4,3,512]{2,1,0:T(4,128)}, bf16[4,512,3,64]{1,3,2,0:T(8,128)(2,1)S(1)}, bf16[2048,3,64]{0,2,1...) while((s32[]{:T(128)}, f32[4,512,3,64]{1,3,2,0:T(8,128)}, ...), condition=%wide.region_3.4_spmd.clone, body=%wide.region_0.3_spmd.clone.sunk | while | flops 2853175808 | bytes 47048840 | solution.py:63
  55.8 2.8 fusion.151
  58.6 15.8 %fusion.152 = f32[4,512,3,64]{1,3,2,0:T(8,128)} fusion(f32[4,512,3,64]{1,3,2,0:T(8,128)} %get-tuple-element.447, s32[]{:T(128)S(6)} %copy.51, f32[2048,3,64]{0,2,1:T(8,128)S(1)} %copy-done.21, f32[3,512,2048]{2,1,0:T(8,128)S(1)} %get-tuple-element.425, f32[3,512]{1,0:T(4,128)S(1)} %fusion.151, f32[3,512]{1,0:T(4,128)S(1)} %get-tuple-element.426, ...), kind=kOutput, calls=%fused_computation.14.clone.1 | convolution fusion | flops 2428502016 | bytes 14563332 | tf_op jit(solution)/shard_map/while/body/eval_jaxpr/while/body/eval_jaxpr/hqk,khd->qhd/dot_general | solution.py:60
  77.7 2.8 fusion.151
  80.5 15.8 %fusion.152 = f32[4,512,3,64]{1,3,2,0:T(8,128)} fusion(f32[4,512,3,64]{1,3,2,0:T(8,128)} %get-tuple-element.447, s32[]{:T(128)S(6)} %copy.51, f32[2048,3,64]{0,2,1:T(8,128)S(1)} %copy-done.21, f32[3,512,2048]{2,1,0:T(8,128)S(1)} %get-tuple-element.425, f32[3,512]{1,0:T(4,128)S(1)} %fusion.151, f32[3,512]{1,0:T(4,128)S(1)} %get-tuple-element.426, ...), kind=kOutput, calls=%fused_computation.14.clone.1 | convolution fusion | flops 2428502016 | bytes 14563332 | tf_op jit(solution)/shard_map/while/body/eval_jaxpr/while/body/eval_jaxpr/hqk,khd->qhd/dot_general | solution.py:60
  99.5 2.8 fusion.151
  102.3 15.8 %fusion.152 = f32[4,512,3,64]{1,3,2,0:T(8,128)} fusion(f32[4,512,3,64]{1,3,2,0:T(8,128)} %get-tuple-element.447, s32[]{:T(128)S(6)} %copy.51, f32[2048,3,64]{0,2,1:T(8,128)S(1)} %copy-done.21, f32[3,512,2048]{2,1,0:T(8,128)S(1)} %get-tuple-element.425, f32[3,512]{1,0:T(4,128)S(1)} %fusion.151, f32[3,512]{1,0:T(4,128)S(1)} %get-tuple-element.426, ...), kind=kOutput, calls=%fused_computation.14.clone.1 | convolution fusion | flops 2428502016 | bytes 14563332 | tf_op jit(solution)/shard_map/while/body/eval_jaxpr/while/body/eval_jaxpr/hqk,khd->qhd/dot_general | solution.py:60
  121.3 2.8 fusion.151
  124.2 15.8 %fusion.152 = f32[4,512,3,64]{1,3,2,0:T(8,128)} fusion(f32[4,512,3,64]{1,3,2,0:T(8,128)} %get-tuple-element.447, s32[]{:T(128)S(6)} %copy.51, f32[2048,3,64]{0,2,1:T(8,128)S(1)} %copy-done.21, f32[3,512,2048]{2,1,0:T(8,128)S(1)} %get-tuple-element.425, f32[3,512]{1,0:T(4,128)S(1)} %fusion.151, f32[3,512]{1,0:T(4,128)S(1)} %get-tuple-element.426, ...), kind=kOutput, calls=%fused_computation.14.clone.1 | convolution fusion | flops 2428502016 | bytes 14563332 | tf_op jit(solution)/shard_map/while/body/eval_jaxpr/while/body/eval_jaxpr/hqk,khd->qhd/dot_general | solution.py:60
  144.5 2.7 fusion.69
  147.3 38.0 %reduce-scatter.5.cloned.1.call-done = bf16[1,512,768]{2,1,0:T(8,128)(2,1)} async-done(((bf16[1,2048,768]{2,1,0:T(8,128)(2,1)}), bf16[1,512,768]{2,1,0:T(8,128)(2,1)}) %reduce-scatter.5.cloned.1.call-update) | async-done | bytes 786448 | tf_op jit(solution)/shard_map/reduce_scatter | solution.py:123
  189.6 28.6 %all-gather.7.cloned.1.call-done = bf16[1,2048,768]{2,1,0:T(8,128)(2,1)} async-done(((bf16[1,512,768]{2,1,0:T(8,128)(2,1)}), bf16[1,2048,768]{2,1,0:T(8,128)(2,1)}) %all-gather.7.cloned.1.call-update) | async-done | bytes 3145744 | tf_op jit(solution)/shard_map/all_gather | solution.py:128
  218.3 5.0 fusion.64
  223.4 5.0 multiply_convert_fusion.3
  230.1 4.0 fusion.70
  234.2 38.1 %reduce-scatter.7.cloned.1.call-done = bf16[1,512,768]{2,1,0:T(8,128)(2,1)} async-done(((bf16[1,2048,768]{2,1,0:T(8,128)(2,1)}), bf16[1,512,768]{2,1,0:T(8,128)(2,1)}) %reduce-scatter.7.cloned.1.call-update) | async-done | bytes 786448 | tf_op jit(solution)/shard_map/reduce_scatter | solution.py:134
  278.1 28.6 %all-gather.9.cloned.1.call-done = bf16[1,2048,768]{2,1,0:T(8,128)(2,1)} async-done(((bf16[1,512,768]{2,1,0:T(8,128)(2,1)}), bf16[1,2048,768]{2,1,0:T(8,128)(2,1)}) %all-gather.9.cloned.1.call-update) | async-done | bytes 3145744 | tf_op jit(solution)/shard_map/all_gather | solution.py:142
  306.7 9.4 %multiply_convert_fusion.1 = (bf16[2048,768]{1,0:T(8,128)(2,1)S(1)}, bf16[2048,768]{1,0:T(8,128)(2,1)S(1)}) fusion(f32[2048,768]{1,0:T(8,128)} %copy-done.46, f32[2048,768]{1,0:T(8,128)} %get-tuple-element.321, bf16[768,768]{1,0:T(8,128)(2,1)S(1)} %copy-done, bf16[1,2048,768]{2,1,0:T(8,128)(2,1)} %all-gather.9.cloned.1.call-done), kind=kOutput, calls=%fused_computation.56 | convolution fusion | flops 2436366336 | bytes 23199744 | tf_op jit(solution)/shard_map/rld,fd->rlf/dot_general | solution.py:145
  316.2 2.7 fusion.102
  318.9 4.1 fusion.71
  323.1 38.1 %reduce-scatter.9.cloned.1.call-done = bf16[1,512,768]{2,1,0:T(8,128)(2,1)} async-done(((bf16[1,2048,768]{2,1,0:T(8,128)(2,1)}), bf16[1,512,768]{2,1,0:T(8,128)(2,1)}) %reduce-scatter.9.cloned.1.call-update) | async-done | bytes 786448 | tf_op jit(solution)/shard_map/reduce_scatter | solution.py:168
  361.2 3.2 multiply_reduce_fusion
  366.6 28.6 %all-gather.11.cloned.1.call-done = bf16[1,2048,768]{2,1,0:T(8,128)(2,1)} async-done(((bf16[1,512,768]{2,1,0:T(8,128)(2,1)}), bf16[1,2048,768]{2,1,0:T(8,128)(2,1)}) %all-gather.11.cloned.1.call-update) | async-done | bytes 3145744 | tf_op jit(solution)/shard_map/all_gather | solution.py:173
  395.2 3.9 fusion.73
  399.1 3.2 reshape.405
  404.5 121.6 %while.49 = (s32[]{:T(128)}, f32[2048,3,64]{0,2,1:T(8,128)S(1)}, f32[2048,3,64]{0,2,1:T(8,128)}, f32[4,512,3,64]{1,0,3,2:T(4,128)}, bf16[4,512,3,64]{1,3,2,0:T(8...) while((s32[]{:T(128)}, f32[2048,3,64]{0,2,1:T(8,128)S(1)}, ...), condition=%wide.region_17.18_spmd.clone, body=%wide.region_15.17_spmd.clone.sunk | while | flops 4059857408 | bytes 74957024 | solution.py:99
  408.8 8.2 fusion.165
  417.1 4.5 multiply_convert_fusion.7
  425.5 8.6 dynamic_update_slice.33
  438.4 9.3 %fusion.165 = f32[2048,3,64]{0,2,1:T(8,128)} fusion(f32[3,512,2048]{2,1,0:T(8,128)S(1)} %fusion.162, f32[3,512]{1,0:T(4,128)S(1)} %dynamic-slice_bitcast_fusion.2, pred[2048]{0:T(1024)(128)(4,1)S(1)} %iota_compare_fusion.5, f32[2048,3,64]{0,2,1:T(8,128)} %get-tuple-element.477, pred[]{:T(512)S(6)} %compare.3, ...), kind=kOutput, calls=%fused_computation.33.clone.1 | convolution fusion | flops 2426142720 | bytes 15935493 | tf_op jit(solution)/shard_map/while/body/eval_jaxpr/while/body/eval_jaxpr/hqk,qhd->khd/dot_general | solution.py:90
  447.7 4.5 multiply_convert_fusion.7
  456.1 8.6 dynamic_update_slice.33
  469.1 9.3 %fusion.165 = f32[2048,3,64]{0,2,1:T(8,128)} fusion(f32[3,512,2048]{2,1,0:T(8,128)S(1)} %fusion.162, f32[3,512]{1,0:T(4,128)S(1)} %dynamic-slice_bitcast_fusion.2, pred[2048]{0:T(1024)(128)(4,1)S(1)} %iota_compare_fusion.5, f32[2048,3,64]{0,2,1:T(8,128)} %get-tuple-element.477, pred[]{:T(512)S(6)} %compare.3, ...), kind=kOutput, calls=%fused_computation.33.clone.1 | convolution fusion | flops 2426142720 | bytes 15935493 | tf_op jit(solution)/shard_map/while/body/eval_jaxpr/while/body/eval_jaxpr/hqk,qhd->khd/dot_general | solution.py:90
  478.4 4.5 multiply_convert_fusion.7
  486.8 8.6 dynamic_update_slice.33
  499.8 9.3 %fusion.165 = f32[2048,3,64]{0,2,1:T(8,128)} fusion(f32[3,512,2048]{2,1,0:T(8,128)S(1)} %fusion.162, f32[3,512]{1,0:T(4,128)S(1)} %dynamic-slice_bitcast_fusion.2, pred[2048]{0:T(1024)(128)(4,1)S(1)} %iota_compare_fusion.5, f32[2048,3,64]{0,2,1:T(8,128)} %get-tuple-element.477, pred[]{:T(512)S(6)} %compare.3, ...), kind=kOutput, calls=%fused_computation.33.clone.1 | convolution fusion | flops 2426142720 | bytes 15935493 | tf_op jit(solution)/shard_map/while/body/eval_jaxpr/while/body/eval_jaxpr/hqk,qhd->khd/dot_general | solution.py:90
  509.0 4.5 multiply_convert_fusion.7
  517.5 8.6 dynamic_update_slice.33
  532.0 4.1 fusion.72
  536.2 7.1 fusion.54
  543.3 4.2 fusion.58
  547.4 4.2 fusion.60
  554.0 3.2 fusion.83
  557.9 39.8 %all-reduce = (f32[768]{0:T(1024)}, f32[768]{0:T(1024)}) all-reduce(f32[768]{0:T(1024)S(1)} %copy-done.31, f32[768]{0:T(1024)S(1)} %copy-done.30), channel_id=1, replica_groups=mesh['rows'=8,'heads'=4] {'rows','heads'}, use_global_device_ids=true, to_apply=%region_25.26 | all-reduce | flops 1536 | bytes 12288 | tf_op jit(solution)/shard_map/psum | solution.py:207
  599.9 281.7 %all-reduce.4.cloned.1.call-done = (f32[3,768,192]{1,2,0:T(8,128)}, f32[192,768]{1,0:T(8,128)}, f32[768,768]{1,0:T(8,128)}, f32[768,768]{1,0:T(8,128)}, f32[768,768]{1,0:T(8,128)}) async-done(((f32[3,768,192]{1,2,0:T(8,128)}, f32[192,768]{1,0:T(8,128)}, f32[768,768]{1,0:T(8,128)}, f32[768,768]{1,0:T(8,128)}, f32[768,768]{1,0:T(8,128)}), (f32[3,768,192]{1,2,0:T(8,128)}, f32[192,768]{1,0:T(8,128)}, ...) | async-done | bytes 9437200 | tf_op jit(solution)/shard_map/psum | solution.py:204
  881.6 2.9 copy.74
  (218 shorter events, 94.5 us)
Async XLA Ops:
  7.2 222.9 %copy-start = (bf16[768,768]{1,0:T(8,128)(2,1)S(1)}, bf16[768,768]{1,0:T(8,128)(2,1)}, u32[]{:S(2)}) copy-start(bf16[768,768]{1,0:T(8,128)(2,1)} %param.20) | copy-start | bytes 3538948
  7.2 33.7 %all-gather.5.cloned.1.call-start = ((), (), s32[]{:S(2)}) async-start(), calls=%async_computation.4 | async-start | bytes 3932160 | tf_op jit(solution)/shard_map/all_gather | solution.py:106
  7.9 177.4 %reduce-scatter.5.cloned.1.call-start = ((), (), s32[]{:S(2)}) async-start(), calls=%async_computation.5 | async-start | bytes 3932160 | tf_op jit(solution)/shard_map/reduce_scatter | solution.py:123
  9.8 35.7 %copy-start.16 = (f32[2048,32]{0,1:T(8,128)}, f32[2048,32]{0,1:T(8,128)S(1)}, u32[]{:S(2)}) copy-start(f32[2048,32]{0,1:T(8,128)S(1)} %get-tuple-element.319) | copy-start | bytes 786436
  45.1 6.5 copy-start.11
  55.8 2.8 copy-start.21
  77.6 2.8 copy-start.21
  99.5 2.8 copy-start.21
  121.3 2.8 copy-start.21
  141.0 2.6 copy-start.4
  141.0 3.5 copy-start.39
  147.2 38.1 %copy-start.2 = (bf16[1,512,768]{2,1,0:T(8,128)(2,1)S(1)}, bf16[1,512,768]{2,1,0:T(8,128)(2,1)}, u32[]{:S(2)}) copy-start(bf16[1,512,768]{2,1,0:T(8,128)(2,1)} %param.14) | copy-start | bytes 2359300
  147.2 41.1 %copy-start.28 = (f32[768]{0:T(1024)S(1)}, f32[768]{0:T(1024)}, u32[]{:S(2)}) copy-start(f32[768]{0:T(1024)} %param.21) | copy-start | bytes 9220
  147.2 71.1 %all-gather.7.cloned.1.call-start = ((), (), s32[]{:S(2)}) async-start(), calls=%async_computation.6 | async-start | bytes 3932160 | tf_op jit(solution)/shard_map/all_gather | solution.py:128
  185.3 3.1 copy-start.3
  189.6 82.7 %reduce-scatter.7.cloned.1.call-start = ((), (), s32[]{:S(2)}) async-start(), calls=%async_computation.7 | async-start | bytes 3932160 | tf_op jit(solution)/shard_map/reduce_scatter | solution.py:134
  218.3 5.1 copy-start.33
  218.3 5.1 copy-start.36
  223.4 5.0 copy-start.46
  234.1 40.3 %copy-start.29 = (f32[768]{0:T(1024)S(1)}, f32[768]{0:T(1024)}, u32[]{:S(2)}) copy-start(f32[768]{0:T(1024)} %param.22) | copy-start | bytes 9220
  234.1 72.6 %all-gather.9.cloned.1.call-start = ((), (), s32[]{:S(2)}) async-start(), calls=%async_computation.8 | async-start | bytes 3932160 | tf_op jit(solution)/shard_map/all_gather | solution.py:142
  278.0 83.1 %reduce-scatter.9.cloned.1.call-start = ((), (), s32[]{:S(2)}) async-start(), calls=%async_computation.9 | async-start | bytes 3932160 | tf_op jit(solution)/shard_map/reduce_scatter | solution.py:168
  306.7 9.5 %copy-start.35 = (bf16[768,768]{1,0:T(8,128)(2,1)S(1)}, bf16[768,768]{1,0:T(8,128)(2,1)}, u32[]{:S(2)}) copy-start(bf16[768,768]{1,0:T(8,128)(2,1)} %param.18) | copy-start | bytes 3538948
  316.1 2.7 copy-start.42
  316.2 2.7 copy-start.44
  316.2 2.7 copy-start.37
  323.0 72.1 %all-gather.11.cloned.1.call-start = ((), (), s32[]{:S(2)}) async-start(), calls=%async_computation.10 | async-start | bytes 3932160 | tf_op jit(solution)/shard_map/all_gather | solution.py:173
  361.2 3.2 copy-start.6
  361.2 3.2 copy-start.15
  364.4 30.8 %copy-start.40 = (bf16[192,768]{1,0:T(8,128)(2,1)S(1)}, bf16[192,768]{1,0:T(8,128)(2,1)}, u32[]{:S(2)}) copy-start(bf16[192,768]{1,0:T(8,128)(2,1)} %param.17) | copy-start | bytes 884740
  366.5 231.2 %reduce-scatter.11.cloned.1.call-start = ((), (), s32[]{:S(2)}) async-start(), calls=%async_computation.11 | async-start | bytes 3932160 | tf_op jit(solution)/shard_map/reduce_scatter | solution.py:200
  399.1 5.4 copy-start.5
  408.8 8.2 copy-start.12
  438.4 9.3 %copy-start.12 = (bf16[2048,3,64]{0,2,1:T(8,128)(2,1)S(1)}, bf16[2048,3,64]{0,2,1:T(8,128)(2,1)}, u32[]{:S(2)}) copy-start(bf16[2048,3,64]{0,2,1:T(8,128)(2,1)} %get-tuple-element.496) | copy-start | bytes 2359300 | tf_op jit(solution)/shard_map/while/body/eval_jaxpr/while
  469.1 9.3 %copy-start.12 = (bf16[2048,3,64]{0,2,1:T(8,128)(2,1)S(1)}, bf16[2048,3,64]{0,2,1:T(8,128)(2,1)}, u32[]{:S(2)}) copy-start(bf16[2048,3,64]{0,2,1:T(8,128)(2,1)} %get-tuple-element.496) | copy-start | bytes 2359300 | tf_op jit(solution)/shard_map/while/body/eval_jaxpr/while
  499.7 9.3 %copy-start.12 = (bf16[2048,3,64]{0,2,1:T(8,128)(2,1)S(1)}, bf16[2048,3,64]{0,2,1:T(8,128)(2,1)}, u32[]{:S(2)}) copy-start(bf16[2048,3,64]{0,2,1:T(8,128)(2,1)} %get-tuple-element.496) | copy-start | bytes 2359300 | tf_op jit(solution)/shard_map/while/body/eval_jaxpr/while
  526.1 4.2 copy-start.17
  536.1 345.5 %all-reduce.4.cloned.1.call-start = ((), (), s32[]{:S(2)}) async-start(), calls=%async_computation.12 | async-start | bytes 18874368 | tf_op jit(solution)/shard_map/psum | solution.py:204
  536.2 7.1 copy-start.34
  536.2 7.1 copy-start.45
  543.2 4.2 copy-start.43
  547.4 4.2 copy-start.9
  547.4 4.2 copy-start.14
  557.2 40.6 %copy-start.7 = (f32[1,512,768]{2,1,0:T(8,128)S(1)}, f32[1,512,768]{2,1,0:T(8,128)}, u32[]{:S(2)}) copy-start(f32[1,512,768]{2,1,0:T(8,128)} %get-tuple-element.293) | copy-start | bytes 4718596
  881.6 3.0 copy-start.27
  881.6 3.8 copy-start.20
  885.4 2.5 copy-start.19
  887.9 3.9 copy-start.1
  (17 other events, 26.3 us)
Sparse Core Ops, SparseCore 0:
  9.6 31.2 all-gather.4
  147.3 37.9 reduce-scatter.4
  189.7 28.5 all-gather.6
  234.2 37.9 reduce-scatter.6
  278.1 28.5 all-gather.8
  323.2 37.9 reduce-scatter.8
  366.6 28.5 all-gather.10
  536.2 38.5 reduce-scatter.10
  580.4 301.1 all-reduce.3
where the time goes:
time: 908 us; the launch traced here: 899 us
  waiting for transfers between devices  514 us (57%)
  matrix products  212 us (23%)
  local copies, waits for them, and re-layouts  68.6 us (8%)
  other arithmetic  49.1 us (5%)
  blocking collectives  39.8 us (4%)
  between operations  14.8 us (2%)
    psum x1, waiting for transfers between devices, on_device(): lax.psum((grad_qkv, grad_out, grad_gate, grad_up, grad_down), 'rows')  282 us
    dot_general x4, matrix products, one_block(): jnp.einsum('hqk,khd->qhd', probs, values_wide, precision=lax.Precision.HI...  63 us
    psum x1, blocking collectives, on_device(): lax.psum((grad_gain_attn, grad_gain_mlp), ('rows', 'heads'))  39.8 us
    reduce_scatter x1, waiting for transfers between devices, on_device(): lax.psum_scatter(mlp_terms.astype(jnp.bfloat16), 'heads', scatter_dimensi...  38.1 us
    reduce_scatter x1, waiting for transfers between devices, on_device(): lax.psum_scatter(normed_terms.astype(jnp.bfloat16), 'heads', scatter_dime...  38.1 us
    reduce_scatter x1, waiting for transfers between devices, on_device(): lax.psum_scatter(attn_terms.astype(jnp.bfloat16), 'heads', scatter_dimens...  38 us
    dynamic_update_slice x8, local copies, waits for them, and re-layouts, attend_row(): results, lse = lax.map(one_block, q_blocks)  36.1 us
    dot_general x4, matrix products, step(): jnp.einsum('hqk,qhd->khd', probs, do_wide, precision=lax.Precision.HIGHEST)  36 us
  transfers between devices with their start and end apart: 9, of which 8 were waited for; matrix products, arithmetic and copies ran while one was open for 3% of the time, Pallas kernels for 0%

commit v1 on v0

v1 whole, which is shorter than its diff:
```python
import functools

import jax
import jax.numpy as jnp
from jax import lax
from jax.experimental import pallas as pl
from jax.experimental.pallas import tpu as pltpu
from jax.sharding import PartitionSpec as P

HEAD = 64
eps = 1e-05
rope_base = 1000.0
MESH = pl.DeviceIdType.MESH
f32 = jnp.float32
bf16 = jnp.bfloat16
NCH = 4


def dot(a, b, ca=1, cb=0):
    return lax.dot_general(a, b, (((ca,), (cb,)), ((), ())), preferred_element_type=f32)


def mean(a):
    return jnp.mean(a, axis=-1, keepdims=True)


def layer_kernel(
    tok, cot, wqt_in, wo_in, wg_in, wu_in, wd_in, ga, gm, cos_t, sin_t, augk,
    out_y, out_dx, g_qkv, g_out, g_gate, g_up, g_down, g_ga, g_gm,
    xall, cotv, wqt, wo, wg, wu, wd, kt, vt, qn, qt, oall, x1b, rown, n1own, inv1own,
    act1, act2, hid, dmb, dab, mrecv, drecv, snd1, snd2, tmp, mtmp, dtmp, itmp,
    dkv, dkvr, dpt, ybuf,
    lsem, wss, wrs, xss, xrs, kss, krs, oss, ors, mss, mrs, bss, brs, dss, drs, ass_, ars,
    css, crs, fss, frs, gss, grs, gls, ysem, credit,
):
    length, width = tok.shape
    cl = length // NCH
    tq = 2 * cl
    ntok = 2 * length
    nkey = 2 * ntok
    qw = wo_in.shape[0]
    hc = qw // HEAD
    nh = 2 * hc
    npair = nh // 2
    fq = wg_in.shape[1]

    h = lax.axis_index("heads")
    x = h // 2
    c = h % 2
    oc = 1 - c
    ox = 1 - x
    core = {"heads": h + 1 - 2 * c}
    xp = {"heads": h + 2 - 4 * x}

    def remote(src, dst, ss, rs, dev):
        return pltpu.make_async_remote_copy(
            src_ref=src, dst_ref=dst, send_sem=ss, recv_sem=rs, device_id=dev, device_id_type=MESH
        )

    barrier = pltpu.get_barrier_semaphore()
    for dev in (core, xp):
        pl.semaphore_signal(barrier, inc=1, device_id=dev, device_id_type=MESH)

    def local_copies():
        cps = []
        for i in range(NCH):
            cps.append(pltpu.make_async_copy(tok.at[pl.ds(i * cl, cl)], xall.at[i, x], lsem.at[i]))
        n = NCH
        for src, dst in (
            (wqt_in, wqt.at[c]), (wo_in, wo.at[x, pl.ds(c * qw, qw)]), (wg_in, wg.at[c]),
            (wu_in, wu.at[c]), (wd_in, wd.at[c]), (cot, cotv),
        ):
            cps.append(pltpu.make_async_copy(src, dst, lsem.at[n]))
            n += 1
        return cps

    locals_ = local_copies()
    for cp in locals_:
        cp.start()

    pl.semaphore_wait(barrier, 2)

    def xcopy(i):
        return remote(tok.at[pl.ds(i * cl, cl)], xall.at[i, x], xss.at[i], xrs.at[i], xp)

    w_q = remote(wqt_in, wqt.at[c], wss.at[0], wrs.at[0], core)
    w_o = remote(wo_in, wo.at[x, pl.ds(c * qw, qw)], wss.at[1], wrs.at[1], core)
    w_ox = remote(wo_in, wo.at[x, pl.ds(c * qw, qw)], wss.at[2], wrs.at[2], xp)
    w_oxc = remote(
        wo.at[ox, pl.ds(c * qw, qw)], wo.at[ox, pl.ds(c * qw, qw)], wss.at[3], wrs.at[3], core
    )
    w_g = remote(wg_in, wg.at[c], wss.at[4], wrs.at[4], core)
    w_u = remote(wu_in, wu.at[c], wss.at[5], wrs.at[5], core)
    w_d = remote(wd_in, wd.at[c], wss.at[6], wrs.at[6], core)
    w_q.start()
    for i in range(NCH):
        xcopy(i).start()
    w_o.start()
    w_g.start()
    w_u.start()
    w_d.start()
    w_ox.start()

    nrow = lax.broadcasted_iota(jnp.int32, (HEAD, nkey), 0)
    vrows = jnp.where(nrow < 2, 1.0, 0.0).astype(bf16)
    for pr in range(npair):
        kt[pr, 0, HEAD:, :] = augk[...]
        kt[pr, 1, :HEAD, :] = augk[...]
        vt[pr, 0, HEAD:, :] = vrows
        vt[pr, 1, :HEAD, :] = vrows
    dkv[...] = jnp.zeros_like(dkv)
    g_ga[...] = jnp.zeros_like(g_ga)
    g_gm[...] = jnp.zeros_like(g_gm)

    lane = lax.broadcasted_iota(jnp.int32, (tq, 2 * HEAD), 1)
    low_half = lane < HEAD

    def rotate(u, cs, sn, sign):
        half = HEAD // 2
        a, b = u[:half], u[half:]
        return jnp.concatenate([a * cs - sign * (b * sn), b * cs + sign * (a * sn)], axis=0)

    def kvcopies(i):
        cps = []
        cols = pl.ds(pl.multiple_of(c * ntok + i * tq, tq), tq)
        n = 0
        for ref in (kt, vt):
            for par in range(2):
                part = ref.at[:, par, pl.ds(par * HEAD, HEAD), cols]
                cps.append(remote(part, part, kss.at[i, n], krs.at[i, n], core))
                n += 1
        return cps

    locals_[NCH].wait()
    w_q.wait_recv()

    def qkv(i, carry):
        pltpu.make_async_copy(tok.at[pl.ds(i * cl, cl)], xall.at[i, x], lsem.at[i]).wait()
        xcopy(i).wait_recv()
        xb = xall[i].reshape(tq, width)
        here = pl.ds(pl.multiple_of(i * tq, tq), tq)
        cols = pl.ds(pl.multiple_of(c * ntok + i * tq, tq), tq)
        cs = cos_t[:, here]
        sn = sin_t[:, here]
        for cc in range(2):
            pt = dot(wqt[cc], xb, 1, 1)
            for j in range(hc):
                hh = cc * hc + j
                pr, par = hh // 2, hh % 2
                at = slice(par * HEAD, par * HEAD + HEAD)
                q = rotate(pt[j * HEAD : (j + 1) * HEAD], cs, sn, 1.0).astype(bf16)
                qt[hh, :, here] = (q.astype(f32) * 0.125).astype(bf16)
                k = rotate(pt[qw + j * HEAD : qw + (j + 1) * HEAD], cs, sn, 1.0)
                kt[pr, par, at, cols] = k.astype(bf16)
                vt[pr, par, at, cols] = pt[2 * qw + j * HEAD : 2 * qw + (j + 1) * HEAD].astype(bf16)
        for cp in kvcopies(i):
            cp.start()
        for pr in range(npair):
            both = jnp.concatenate([qt[2 * pr, :, here], qt[2 * pr + 1, :, here]], axis=0)
            nat = both.astype(f32).T
            qn[2 * pr, here, :] = jnp.where(
                low_half, nat, jnp.where(lane == HEAD, 1.0, 0.0)
            ).astype(bf16)
            qn[2 * pr + 1, here, :] = jnp.where(
                low_half, jnp.where(lane == 0, 1.0, 0.0), nat
            ).astype(bf16)
        return carry

    lax.fori_loop(0, NCH, qkv, 0)

    def kvwait(i, carry):
        for cp in kvcopies(i):
            cp.wait_recv()
        return carry

    lax.fori_loop(0, NCH, kvwait, 0)
    w_ox.wait_recv()
    w_oxc.start()
    for cp in locals_[NCH + 1 :]:
        cp.wait()
    for w in (w_o, w_oxc, w_g, w_u, w_d):
        w.wait_recv()

    def rows_of(i):
        return pl.ds(pl.multiple_of(i * tq, tq), tq)

    def own_of(i):
        return pl.ds(pl.multiple_of(i * cl, cl), cl)

    def ocopy(i):
        part = oall.at[x, rows_of(i)]
        return remote(part, part, oss.at[i], ors.at[i], xp)

    def mcopy(i):
        return remote(snd1.at[i], mrecv.at[i], mss.at[i], mrs.at[i], xp)

    def bcopy(i):
        return remote(dmb.at[i, x], dmb.at[i, x], bss.at[i], brs.at[i], xp)

    def dcopy(i):
        return remote(snd2.at[i], drecv.at[i], dss.at[i], drs.at[i], xp)

    def acopy(i):
        return remote(dab.at[i, x], dab.at[i, x], ass_.at[i], ars.at[i], xp)

    def ycopy(i):
        return pltpu.make_async_copy(ybuf.at[i], out_y.at[pl.ds(i * cl, cl)], ysem.at[i])

    def attend(i):
        rows = rows_of(i)
        for pr in range(npair):
            outs = []
            for par in range(2):
                hh = 2 * pr + par
                base = HEAD * (1 - par)
                qq = qn[hh, rows, :]
                s = dot(qq, kt[pr, par])
                top = jnp.max(s, axis=1, keepdims=True)
                p = jnp.exp(s - top).astype(bf16)
                oo = dot(p, vt[pr, par], 1, 1)
                total = oo[:, base : base + 1]
                outs.append(oo * (1.0 / total))
                neg = -(top + jnp.log(total))
                hi = neg.astype(bf16).astype(f32)
                mid = (neg - hi).astype(bf16).astype(f32)
                lo = neg - hi - mid
                qf = qq.astype(f32)
                qf = jnp.where(lane == base + 1, hi, qf)
                qf = jnp.where(lane == base + 2, mid, qf)
                qf = jnp.where(lane == base + 3, lo, qf)
                qn[hh, rows, :] = qf.astype(bf16)
            oall[x, rows, pr * 2 * HEAD : (pr + 1) * 2 * HEAD] = jnp.where(
                low_half, outs[0], outs[1]
            ).astype(bf16)
        ocopy(i).start()

    def mlp_fwd(i):
        rows, own = rows_of(i), own_of(i)
        ocopy(i).wait_recv()
        a = dot(oall[0, rows, :], wo[0]) + dot(oall[1, rows, :], wo[1])
        r = xall[i].reshape(tq, width).astype(f32) + a
        centre = r - mean(r)
        inv = lax.rsqrt(mean(centre * centre) + eps)
        n1 = centre * inv
        tmp[...] = n1.reshape(2, cl, width)
        n1own[own, :] = tmp[x]
        itmp[...] = jnp.broadcast_to(inv, (tq, 128)).reshape(2, cl, 128)
        inv1own[own, :] = itmp[x]
        x1 = n1 * ga[...]
        tmp[...] = x1.reshape(2, cl, width)
        rown[own, :] = tmp[x]
        xb = x1.astype(bf16)
        x1b[rows, :] = xb
        m = None
        for cc in range(2):
            g = dot(xb, wg[cc])
            u = dot(xb, wu[cc])
            sg = 0.5 * jnp.tanh(0.5 * g) + 0.5
            si = g * sg
            hv = (si * u).astype(bf16)
            act2[cc, rows, :] = si.astype(bf16)
            act1[cc, rows, :] = (u * (sg + si * (1.0 - sg))).astype(bf16)
            hid[cc, rows, :] = hv
            part = dot(hv, wd[cc])
            m = part if m is None else m + part
        mtmp[...] = m.reshape(2, cl, width)
        snd1[i] = mtmp[ox].astype(bf16)
        mcopy(i).start()

    def norm_two(i):
        own = own_of(i)
        mcopy(i).wait_recv()
        r = rown[own, :] + (mtmp[x] + mrecv[i].astype(f32))
        centre = r - mean(r)
        inv = lax.rsqrt(mean(centre * centre) + eps)
        n2 = centre * inv
        ybuf[i] = (n2 * gm[...]).astype(bf16)
        ycopy(i).start()
        dy = cotv[own, :].astype(f32)
        g_gm[...] += jnp.sum(dy * n2, axis=0, keepdims=True)
        e = dy * gm[...]
        dr = inv * (e - mean(e) - n2 * mean(e * n2))
        rown[own, :] = dr
        dmb[i, x] = dr.astype(bf16)
        bcopy(i).start()

    def mlp_bwd(i):
        rows = rows_of(i)
        bcopy(i).wait_recv()
        db = dmb[i].reshape(tq, width)
        d = None
        for cc in range(2):
            dh = dot(db, wd[cc], 1, 1)
            dg = (dh * act1[cc, rows, :].astype(f32)).astype(bf16)
            du = (dh * act2[cc, rows, :].astype(f32)).astype(bf16)
            act1[cc, rows, :] = dg
            act2[cc, rows, :] = du
            part = dot(dg, wg[cc], 1, 1) + dot(du, wu[cc], 1, 1)
            d = part if d is None else d + part
        dtmp[...] = d.reshape(2, cl, width)
        snd2[i] = dtmp[ox].astype(bf16)
        dcopy(i).start()

    def norm_one(i):
        own = own_of(i)
        dcopy(i).wait_recv()
        dx = rown[own, :] + (dtmp[x] + drecv[i].astype(f32))
        n1 = n1own[own, :]
        g_ga[...] += jnp.sum(dx * n1, axis=0, keepdims=True)
        e = dx * ga[...]
        dr = inv1own[own, 0:1] * (e - mean(e) - n1 * mean(e * n1))
        rown[own, :] = dr
        dab[i, x] = dr.astype(bf16)
        acopy(i).start()

    kb = min(1024, nkey)

    def attend_back(i):
        rows = rows_of(i)
        acopy(i).wait_recv()
        da = dab[i].reshape(tq, width)
        cs = cos_t[:, rows]
        sn = sin_t[:, rows]
        wox = wo[x]
        for pr in range(npair):
            pair = slice(pr * 2 * HEAD, (pr + 1) * 2 * HEAD)
            dop = dot(da, wox[pair], 1, 1).astype(bf16)
            dof = dop.astype(f32)
            prod = dof * oall[x, rows, pair].astype(f32)
            dot_t = dof.T.astype(bf16)
            dqs = []
            for par in range(2):
                hh = 2 * pr + par
                base = HEAD * (1 - par)
                mine = low_half if par == 0 else jnp.logical_not(low_half)
                neg = -jnp.sum(jnp.where(mine, prod, 0.0), axis=1, keepdims=True)
                hi = neg.astype(bf16).astype(f32)
                lo = neg - hi
                aug = jnp.where(lane == base, hi, jnp.where(lane == base + 1, lo, 0.0))
                doa = jnp.where(mine, dof, aug).astype(bf16)
                qq = qn[hh, rows, :]
                dq = None
                for b in range(nkey // kb):
                    kk = slice(b * kb, (b + 1) * kb)
                    p = jnp.exp(dot(qq, kt[pr, par, :, kk]))
                    d = dot(doa, vt[pr, par, :, kk])
                    ds = (p * d).astype(bf16)
                    pb = p.astype(bf16)
                    dkv[1, hh, :, kk] += dot(dot_t[par * HEAD : (par + 1) * HEAD], pb)
                    dkv[0, hh, :, kk] += dot(qt[hh, :, rows], ds)
                    part = dot(ds, kt[pr, par, :, kk], 1, 1)
                    dq = part if dq is None else dq + part
                dqs.append(dq)
            dqt = jnp.where(low_half, dqs[0], dqs[1]).T * 0.125
            for par in range(2):
                hh = 2 * pr + par
                cc, j = hh // hc, hh % hc
                u = rotate(dqt[par * HEAD : (par + 1) * HEAD], cs, sn, -1.0)
                dpt[cc, j * HEAD : (j + 1) * HEAD, rows] = u.astype(bf16)

    stages = (attend, mlp_fwd, norm_two, mlp_bwd, norm_one, attend_back)

    def step(t, carry):
        for lag in reversed(range(len(stages))):
            stage = stages[lag]

            @pl.when(jnp.logical_and(t >= lag, t < NCH + lag))
            def _():
                stage(t - lag)

        return carry

    lax.fori_loop(0, NCH + len(stages) - 1, step, 0)

    def give_credit(n):
        pl.semaphore_signal(credit.at[n], inc=1, device_id=core, device_id_type=MESH)

    blk = pl.ds(0, fq)
    out_rows = pl.ds(0, qw)
    qkv_rows = pl.ds(qw, 3 * qw)
    g_plan = (
        (wg.at[0], wg.at[1], wd.at[1], g_gate),
        (wu.at[0], wu.at[1], act1.at[0, blk], g_up),
        (wd.at[0], act1.at[1, blk], act2.at[0, blk], g_down),
        (act2.at[1, out_rows], hid.at[1, out_rows], hid.at[0, out_rows], g_out),
        (act2.at[1, qkv_rows], hid.at[1, qkv_rows], hid.at[0, qkv_rows], g_qkv),
    )

    def gcopy(n):
        return remote(g_plan[n][2], g_plan[n][1], gss.at[n], grs.at[n], core)

    def gstore(n):
        return pltpu.make_async_copy(g_plan[n][0], g_plan[n][3], gls.at[n])

    def gsum(n):
        gcopy(n).wait()
        mine, got = g_plan[n][:2]
        mine[...] = (mine[...].astype(f32) + got[...].astype(f32)).astype(bf16)
        gstore(n).start()

    dmball = dmb[...].reshape(ntok, width)
    g_plan[0][2][...] = dot(x1b[...], act1[oc], 0, 0).astype(bf16)
    g_plan[0][0][...] = dot(x1b[...], act1[c], 0, 0).astype(bf16)
    give_credit(0)
    pl.semaphore_wait(credit.at[0], 1)
    gcopy(0).start()
    g_plan[1][2][...] = dot(x1b[...], act2[oc], 0, 0).astype(bf16)
    gcopy(1).start()
    g_plan[1][0][...] = dot(x1b[...], act2[c], 0, 0).astype(bf16)
    g_plan[2][2][...] = dot(hid[oc], dmball, 0, 0).astype(bf16)
    gcopy(2).start()
    g_plan[2][0][...] = dot(hid[c], dmball, 0, 0).astype(bf16)
    give_credit(1)
    pl.semaphore_wait(credit.at[1], 1)
    for n in range(3):
        gsum(n)

    theirs = pl.ds(pl.multiple_of(oc * ntok, ntok), ntok)
    mine_cols = pl.ds(pl.multiple_of(c * ntok, ntok), ntok)
    for hh in range(nh):
        cc, j = hh // hc, hh % hc
        for n in range(2):
            at = slice((n + 1) * qw + j * HEAD, (n + 1) * qw + (j + 1) * HEAD)
            dpt[cc, at, :] = dkv[n, hh, :, theirs].astype(bf16)
    kvback = remote(dpt.at[:, pl.ds(qw, 2 * qw)], dkvr, css.at[0], crs.at[0], core)
    kvback.start()

    daball = dab[...].reshape(ntok, width)
    o = oall[x]
    part_a = dot(o[:, :qw], daball, 0, 0)
    part_b = dot(o[:, qw:], daball, 0, 0)
    g_plan[3][2][...] = jnp.where(oc == 0, part_a, part_b).astype(bf16)
    gcopy(3).start()
    g_plan[3][0][...] = jnp.where(c == 0, part_a, part_b).astype(bf16)

    kvback.wait()
    for hh in range(nh):
        cc, j = hh // hc, hh % hc
        for n in range(2):
            at = slice((n + 1) * qw + j * HEAD, (n + 1) * qw + (j + 1) * HEAD)
            got = slice(n * qw + j * HEAD, n * qw + (j + 1) * HEAD)
            u = dkv[n, hh, :, mine_cols] + dkvr[cc, got].astype(f32)
            if n == 0:
                u = rotate(u, cos_t[...], sin_t[...], -1.0)
            dpt[cc, at, :] = u.astype(bf16)

    def fcopy(i):
        return remote(snd1.at[i], mrecv.at[i], fss.at[i], frs.at[i], xp)

    def input_terms(i, who):
        cols = pl.ds(pl.multiple_of(i * tq + who * cl, cl), cl)
        d = None
        for cc in range(2):
            part = dot(dpt[cc, :, cols], wqt[cc], 0, 0)
            d = part if d is None else d + part
        return d

    for i in range(NCH):
        mcopy(i).wait_send()
        snd1[i] = input_terms(i, ox).astype(bf16)
        fcopy(i).start()

    xr = xall[...].reshape(ntok, width)
    g_plan[4][2][...] = dot(dpt[oc], xr).astype(bf16)
    gcopy(4).start()
    g_plan[4][0][...] = dot(dpt[c], xr).astype(bf16)
    gsum(3)
    gsum(4)

    for i in range(NCH):
        d = input_terms(i, x)
        fcopy(i).wait_recv()
        own = pl.ds(i * cl, cl)
        d = rown[own, :] + (d + mrecv[i].astype(f32))
        ycopy(i).wait()
        ybuf[i] = d.astype(bf16)
        pltpu.make_async_copy(ybuf.at[i], out_dx.at[own], lsem.at[i]).start()

    for i in range(NCH):
        own = pl.ds(i * cl, cl)
        pltpu.make_async_copy(ybuf.at[i], out_dx.at[own], lsem.at[i]).wait()
        xcopy(i).wait_send()
        for cp in kvcopies(i):
            cp.wait_send()
        ocopy(i).wait_send()
        bcopy(i).wait_send()
        dcopy(i).wait_send()
        acopy(i).wait_send()
        fcopy(i).wait_send()
    for w in (w_q, w_o, w_ox, w_oxc, w_g, w_u, w_d):
        w.wait_send()
    for n in range(len(g_plan)):
        gstore(n).wait()


def on_device(tokens, lengths, w_qkv, w_out, w_gate, w_up, w_down, gain_attn, gain_mlp, cotangent):
    _, length, width = tokens.shape
    qw = w_qkv.shape[2]
    fq = w_gate.shape[1]
    nh = 2 * qw // HEAD
    cl = length // NCH
    tq = 2 * cl
    ntok = 2 * length
    nkey = 2 * ntok
    h = lax.axis_index("heads")
    c = h % 2

    order = jnp.arange(nkey, dtype=jnp.int32).reshape(2, NCH, 2, cl)
    cores = lax.broadcasted_iota(jnp.int32, order.shape, 0)
    chunk = lax.broadcasted_iota(jnp.int32, order.shape, 1)
    xs = lax.broadcasted_iota(jnp.int32, order.shape, 2)
    place = lax.broadcasted_iota(jnp.int32, order.shape, 3)
    position = (2 * xs + cores) * length + chunk * cl + place
    valid = position.reshape(1, nkey) < lengths[0]
    row = lax.broadcasted_iota(jnp.int32, (HEAD, nkey), 0)
    augk = jnp.where(
        row == 0, jnp.where(valid, 0.0, -1e30), jnp.where(row < 4, 1.0, 0.0)
    ).astype(bf16)
    here = ((2 * xs[0] + c) * length + chunk[0] * cl + place[0]).reshape(1, ntok).astype(f32)
    half = HEAD // 2
    freqs = rope_base ** (-jnp.arange(half).astype(f32) / half)
    angles = freqs[:, None] * here
    cos_t, sin_t = jnp.cos(angles), jnp.sin(angles)

    wqt = w_qkv.transpose(0, 2, 1).reshape(3 * qw, width)

    hbm = pl.BlockSpec(memory_space=pl.ANY)
    vmem = pl.BlockSpec(memory_space=pltpu.VMEM)
    S = jax.ShapeDtypeStruct
    V = pltpu.VMEM
    dma = pltpu.SemaphoreType.DMA
    fc = 2 * fq
    scratch = [
        V((NCH, 2, cl, width), bf16),
        V((length, width), bf16),
        V((2, 3 * qw, width), bf16),
        V((2, 2 * qw, width), bf16),
        V((2, width, fq), bf16),
        V((2, width, fq), bf16),
        V((2, fq, width), bf16),
        V((nh // 2, 2, 2 * HEAD, nkey), bf16),
        V((nh // 2, 2, 2 * HEAD, nkey), bf16),
        V((nh, ntok, 2 * HEAD), bf16),
        V((nh, HEAD, ntok), bf16),
        V((2, ntok, 2 * qw), bf16),
        V((ntok, width), bf16),
        V((length, width), f32),
        V((length, width), f32),
        V((length, 128), f32),
        V((2, ntok, fq), bf16),
        V((2, ntok, fq), bf16),
        V((2, ntok, fq), bf16),
        V((NCH, 2, cl, width), bf16),
        V((NCH, 2, cl, width), bf16),
        V((NCH, cl, width), bf16),
        V((NCH, cl, width), bf16),
        V((NCH, cl, width), bf16),
        V((NCH, cl, width), bf16),
        V((2, cl, width), f32),
        V((2, cl, width), f32),
        V((2, cl, width), f32),
        V((2, cl, 128), f32),
        V((2, nh, HEAD, nkey), f32),
        V((2, 2 * qw, ntok), bf16),
        V((2, 3 * qw, ntok), bf16),
        V((NCH, cl, width), bf16),
        dma((NCH + 6,)),
        dma((7,)), dma((7,)),
        dma((NCH,)), dma((NCH,)),
        dma((NCH, 4)), dma((NCH, 4)),
        dma((NCH,)), dma((NCH,)),
        dma((NCH,)), dma((NCH,)),
        dma((NCH,)), dma((NCH,)),
        dma((NCH,)), dma((NCH,)),
        dma((NCH,)), dma((NCH,)),
        dma((1,)), dma((1,)),
        dma((NCH,)), dma((NCH,)),
        dma((5,)), dma((5,)), dma((5,)),
        dma((NCH,)),
        pltpu.SemaphoreType.REGULAR((2,)),
    ]
    outs = pl.pallas_call(
        layer_kernel,
        out_shape=[
            S((length, width), bf16), S((length, width), bf16),
            S((3 * qw, width), bf16), S((qw, width), bf16),
            S((width, fq), bf16), S((width, fq), bf16), S((fq, width), bf16),
            S((1, width), f32), S((1, width), f32),
        ],
        in_specs=[hbm] * 7 + [vmem] * 5,
        out_specs=[hbm] * 7 + [vmem] * 2,
        scratch_shapes=scratch,
        compiler_params=pltpu.CompilerParams(
            collective_id=0, has_side_effects=True, vmem_limit_bytes=VLIM
        ),
    )(
        tokens[0], cotangent[0], wqt, w_out, w_gate, w_up, w_down,
        gain_attn[None], gain_mlp[None], cos_t, sin_t, augk,
    )
    y, dx, gqt, go, gg, gu, gd, gga, ggm = outs
    gqt, go, gg, gu, gd = lax.psum((gqt, go, gg, gu, gd), "rows")
    gga, ggm = lax.psum((gga, ggm), ("rows", "heads"))
    grad_qkv = gqt.astype(f32).reshape(3, qw, width).transpose(0, 2, 1)
    return (
        y[None], dx[None], grad_qkv, go.astype(f32), gg.astype(f32), gu.astype(f32),
        gd.astype(f32), gga[0], ggm[0],
    )


VLIM = 64 * 2**20


def solution(mesh):
    in_specs = (
        P("rows", "heads", None),
        P("rows"),
        P(None, None, "heads"),
        P("heads", None),
        P(None, "heads"),
        P(None, "heads"),
        P("heads", None),
        P(),
        P(),
        P("rows", "heads", None),
    )
    out_specs = (
        P("rows", "heads", None),
        P("rows", "heads", None),
        P(None, None, "heads"),
        P("heads", None),
        P(None, "heads"),
        P(None, "heads"),
        P("heads", None),
        P(),
        P(),
    )
    return jax.shard_map(
        on_device, mesh=mesh, in_specs=in_specs, out_specs=out_specs, check_vma=False
    )
```

time: 908 us -> 382 us (0.42); the launches traced: 899 us -> 382 us
  waiting for transfers between devices: 514 us -> 129 us
  matrix products: 212 us -> 0 us
  Pallas kernels: 0 us -> 180 us
  local copies, waits for them, and re-layouts: 68.6 us -> 5.06 us
  other arithmetic: 49.1 us -> 10.5 us
    dot_general x43 -> x0, matrix products: 212 us -> none  [the longest x4 63 us: one_block(): jnp.einsum('hqk,khd->qhd', probs, values_wide, precision=lax.Precision.HI...]
    pallas_call x0 -> x1, Pallas kernels: none -> 180 us  [on_device(): pl.pallas_call(layer_kernel, out_shape=[S((length, width), bf16), S((leng...]
    psum x1, waiting for transfers between devices: 282 us -> 129 us  [on_device(): gqt, go, gg, gu, gd = lax.psum((gqt, go, gg, gu, gd), 'rows')]
    all_gather x4 -> x0, waiting for transfers between devices: 117 us -> none  [the longest x1 31 us: on_device(): whole = lax.all_gather(tokens, 'heads', axis=1, tiled=True)]
    reduce_scatter x4 -> x0, waiting for transfers between devices: 114 us -> none  [the longest x1 38.1 us: on_device(): lax.psum_scatter(mlp_terms.astype(jnp.bfloat16), 'heads', scatter_dimensi...]
    dynamic_update_slice x8 -> x0, local copies, waits for them, and re-layouts: 36.1 us -> none  [attend_row(): results, lse = lax.map(one_block, q_blocks)]
    reduce_sum x14 -> x0, other arithmetic: 25.4 us -> none  [the longest x4 11.3 us: one_block(): total = jnp.sum(expo, axis=2, keepdims=True)]
    unnamed x96 -> x18, local copies, waits for them, and re-layouts: 19.6 us -> 2.52 us
  transfers between devices with their start and end apart: 9 -> 1, of which waited for: 8 -> 1; matrix products, arithmetic and copies ran while one was open for 3% -> 0% of each run, Pallas kernels for 0% -> 0%
where the time goes in v1:
time: 382 us
  Pallas kernels  180 us (47%)
  waiting for transfers between devices  129 us (34%)
  blocking collectives  42.3 us (11%)
  between operations  14.8 us (4%)
  other arithmetic  10.5 us (3%)
  local copies, waits for them, and re-layouts  5.06 us (1%)
    pallas_call x1, Pallas kernels, on_device(): pl.pallas_call(layer_kernel, out_shape=[S((length, width), bf16), S((leng...  180 us
    psum x1, waiting for transfers between devices, on_device(): gqt, go, gg, gu, gd = lax.psum((gqt, go, gg, gu, gd), 'rows')  129 us
    psum x1, blocking collectives, on_device(): gga, ggm = lax.psum((gga, ggm), ('rows', 'heads'))  42.3 us
  transfers between devices with their start and end apart: 1, of which 1 were waited for; matrix products, arithmetic and copies ran while one was open for 0% of the time, Pallas kernels for 0%

profile of v1, /device:TPU:0, one launch (start us, length us, event | category | flops | bytes accessed | tf_op | source)
XLA Modules:
  0.0 381.9 jit_solution(13530944799348212916)
XLA Ops:
  7.2 0.0 all-reduce.4.cloned.1.call-start
  8.0 1.3 broadcast_in_dim.37.ga
  9.2 1.3 broadcast_in_dim.38.gm
  10.5 1.2 multiply_sine_fusion
  11.7 0.1 compare_select_fusion
  11.8 0.8 select_convert_fusion.augk
  12.6 179.9 %shard_map.169 = (bf16[512,768]{1,0:T(8,128)(2,1)}, bf16[512,768]{1,0:T(8,128)(2,1)}, bf16[576,768]{1,0:T(8,128)(2,1)}, bf16[192,768]{1,0:T(8,128)(2,1)}, bf16[7...) custom-call(bf16[512,768]{1,0:T(8,128)(2,1)} %bitcast.19, ...), custom_call_target="tpu_custom_call" | custom-call | tf_op jit(solution)/shard_map/pallas_call | solution.py:582
  192.6 0.0 copy-start.7
  192.6 0.0 copy-start.6
  192.6 0.0 all-reduce.4.cloned.1.call-update
  192.6 0.6 copy-done.7
  193.3 0.0 copy-done.6
  193.3 42.3 %all-reduce = (f32[768]{0:T(1024)}, f32[768]{0:T(1024)}) all-reduce(f32[768]{0:T(1024)S(1)} %reduce, f32[768]{0:T(1024)S(1)} %reduce.1), channel_id=1, replica_groups=mesh['rows'=8,'heads'=4] {'rows','heads'}, use_global_device_ids=true, to_apply=%region_5.6 | all-reduce | flops 1536 | bytes 12288 | tf_op jit(solution)/shard_map/psum | solution.py:602
  235.6 129.3 %all-reduce.4.cloned.1.call-done = (bf16[3,768,192]{1,2,0:T(8,128)(2,1)}, bf16[192,768]{1,0:T(8,128)(2,1)}, bf16[768,768]{1,0:T(8,128)(2,1)}, bf16[768,768]{1,0:T(8,128)(2,1)}, bf16[768,768]{1,0:T(8,128)(2,1)}) async-done(((bf16[3,768,192]{1,2,0:T(8,128)(2,1)}, bf16[192,768]{1,0:T(8,128)(2,1)}, bf16[768,768]{1,0:T(8,128)(2,1)}, bf16[768,768]{1,0:T(8,128)(2,1)}, bf16[768,768]{1,0:T(8,128)(2,1)}), ...) | async-done | bytes 4718608 | tf_op jit(solution)/shard_map/psum | solution.py:601
  364.9 0.0 copy-start.1
  364.9 2.9 convert_element_type.35
  367.9 0.0 copy-done.1
  367.9 0.0 copy-start
  367.9 1.6 convert_element_type.36
  369.4 0.1 copy-done
  369.5 0.0 copy-start.2
  369.5 1.6 convert_element_type.37
  371.1 0.0 copy-done.2
  371.1 0.0 copy-start.5
  371.1 0.0 copy-start.4
  371.1 1.4 transpose.15
  372.5 0.0 copy-done.5
  372.5 0.0 copy-start.3
  372.5 0.9 convert_element_type.34
  373.3 0.0 copy-done.4
  373.3 0.9 copy.27
  374.2 0.0 copy-done.3
  374.2 0.9 copy.28
  (10 shorter events, 0.1 us)
Async XLA Ops:
  7.2 357.7 %all-reduce.4.cloned.1.call-start = ((), (), s32[]{:S(2)}) async-start(), calls=%async_computation | async-start | bytes 9437184 | tf_op jit(solution)/shard_map/psum | solution.py:601
  192.6 0.7 copy-start.7
  192.6 0.7 copy-start.6
  364.9 2.9 copy-start.1
  367.9 1.7 copy-start
  369.5 1.6 copy-start.2
  371.1 1.4 copy-start.5
  371.1 2.2 copy-start.4
  372.5 1.7 copy-start.3
Sparse Core Ops, SparseCore 0:
  192.7 172.1 all-reduce.3

commit v2 on v1

v2 whole, which is shorter than its diff:
```python
import functools

import jax
import jax.numpy as jnp
from jax import lax
from jax.experimental import pallas as pl
from jax.experimental.pallas import tpu as pltpu
from jax.sharding import PartitionSpec as P

HEAD = 64
eps = 1e-05
rope_base = 1000.0
MESH = pl.DeviceIdType.MESH
f32 = jnp.float32
bf16 = jnp.bfloat16
NCH = 4


def dot(a, b, ca=1, cb=0):
    return lax.dot_general(a, b, (((ca,), (cb,)), ((), ())), preferred_element_type=f32)


def mean(a):
    return jnp.mean(a, axis=-1, keepdims=True)


def layer_kernel(
    nrows, tok, cot, wqt_in, wo_in, wg_in, wu_in, wd_in, ga, gm, cos_t, sin_t, augk,
    out_y, out_dx, g_mlp, g_att, g_gain,
    xall, cotv, wqt, wo, wm, kt, vt, qn, qt, oall, x1b, rown, n1own, inv1own,
    act1, act2, hid, dmb, dab, mrecv, drecv, snd1, snd2, tmp, mtmp, dtmp, itmp,
    dkv, dkvr, dpt, ybuf, gsent, agrad, gbuf, grecv,
    lsem, wss, wrs, xss, xrs, kss, krs, oss, ors, mss, mrs, bss, brs, dss, drs, ass_, ars,
    css, crs, fss, frs, gss, grs, gls, rss, rrs, fas, far, ns, nr, ysem, credit,
):
    ring = nrows == 8
    length, width = tok.shape
    cl = length // NCH
    tq = 2 * cl
    ntok = 2 * length
    nkey = 2 * ntok
    hc = wo_in.shape[0]
    qw = hc * HEAD
    fq = wg_in.shape[1]

    h = lax.axis_index("heads")
    r = lax.axis_index("rows")
    x = h // 2
    c = h % 2
    oc = 1 - c
    ox = 1 - x
    core = {"heads": h + 1 - 2 * c}
    xp = {"heads": h + 2 - 4 * x}
    y = r % 2
    z = r // 2
    outer = jnp.logical_or(z == 0, z == 3)
    inner = jnp.logical_not(outer)
    ydev = {"rows": r + 1 - 2 * y}
    zdev = {"rows": r + 2 - 4 * (z % 2)}
    mid = {"rows": (3 - z) * 2 + y}
    doubling = [core, xp]
    span = 1
    while span < nrows:
        doubling.append({"rows": r + span - 2 * span * ((r // span) % 2)})
        span *= 2

    def when(cond):
        return pl.when(cond)

    def remote(src, dst, ss, rs, dev):
        return pltpu.make_async_remote_copy(
            src_ref=src, dst_ref=dst, send_sem=ss, recv_sem=rs, device_id=dev, device_id_type=MESH
        )

    barrier = pltpu.get_barrier_semaphore()
    for dev in doubling:
        pl.semaphore_signal(barrier, inc=1, device_id=dev, device_id_type=MESH)
    greeted = len(doubling)
    if ring:

        @when(inner)
        def _():
            pl.semaphore_signal(barrier, inc=1, device_id=mid, device_id_type=MESH)

        greeted = greeted + jnp.where(inner, 1, 0)

    def local_copies():
        cps = []
        for i in range(NCH):
            cps.append(pltpu.make_async_copy(tok.at[pl.ds(i * cl, cl)], xall.at[i, x], lsem.at[i]))
        n = NCH
        for src, dst in (
            (wqt_in, wqt.at[c]), (wo_in, wo.at[x, :, c]), (wg_in, wm.at[3 * c]),
            (wu_in, wm.at[3 * c + 1]), (wd_in, wm.at[3 * c + 2]), (cot, cotv),
        ):
            cps.append(pltpu.make_async_copy(src, dst, lsem.at[n]))
            n += 1
        return cps

    locals_ = local_copies()
    for cp in locals_:
        cp.start()

    pl.semaphore_wait(barrier, greeted)

    def xcopy(i):
        return remote(tok.at[pl.ds(i * cl, cl)], xall.at[i, x], xss.at[i], xrs.at[i], xp)

    w_q = remote(wqt_in, wqt.at[c], wss.at[0], wrs.at[0], core)
    w_o = remote(wo_in, wo.at[x, :, c], wss.at[1], wrs.at[1], core)
    w_ox = remote(wo_in, wo.at[x, :, c], wss.at[2], wrs.at[2], xp)
    w_oxc = remote(wo.at[ox, :, c], wo.at[ox, :, c], wss.at[3], wrs.at[3], core)
    w_g = remote(wg_in, wm.at[3 * c], wss.at[4], wrs.at[4], core)
    w_u = remote(wu_in, wm.at[3 * c + 1], wss.at[5], wrs.at[5], core)
    w_d = remote(wd_in, wm.at[3 * c + 2], wss.at[6], wrs.at[6], core)
    w_q.start()
    for i in range(NCH):
        xcopy(i).start()
    w_o.start()
    w_g.start()
    w_u.start()
    w_d.start()
    w_ox.start()

    nrow = lax.broadcasted_iota(jnp.int32, (HEAD, nkey), 0)
    vrows = jnp.where(nrow < 2, 1.0, 0.0).astype(bf16)
    for pr in range(hc):
        kt[pr, 0, HEAD:, :] = augk[...]
        kt[pr, 1, :HEAD, :] = augk[...]
        vt[pr, 0, HEAD:, :] = vrows
        vt[pr, 1, :HEAD, :] = vrows
    gbuf[...] = jnp.zeros_like(gbuf)

    lane = lax.broadcasted_iota(jnp.int32, (tq, 2 * HEAD), 1)
    low_half = lane < HEAD

    def rotate(u, cs, sn, sign):
        half = HEAD // 2
        a, b = u[:half], u[half:]
        return jnp.concatenate([a * cs - sign * (b * sn), b * cs + sign * (a * sn)], axis=0)

    def kvcopies(i):
        cps = []
        cols = pl.ds(pl.multiple_of(c * ntok + i * tq, tq), tq)
        n = 0
        for ref in (kt, vt):
            for par in range(2):
                part = ref.at[:, par, pl.ds(par * HEAD, HEAD), cols]
                cps.append(remote(part, part, kss.at[i, n], krs.at[i, n], core))
                n += 1
        return cps

    locals_[NCH].wait()
    w_q.wait_recv()

    def qkv(i, carry):
        pltpu.make_async_copy(tok.at[pl.ds(i * cl, cl)], xall.at[i, x], lsem.at[i]).wait()
        xcopy(i).wait_recv()
        xb = xall[i].reshape(tq, width)
        here = pl.ds(pl.multiple_of(i * tq, tq), tq)
        cols = pl.ds(pl.multiple_of(c * ntok + i * tq, tq), tq)
        cs = cos_t[:, here]
        sn = sin_t[:, here]
        for cc in range(2):
            pt = dot(wqt[cc], xb, 1, 1)
            at = slice(cc * HEAD, cc * HEAD + HEAD)
            for j in range(hc):
                u = pt[j * 3 * HEAD : (j + 1) * 3 * HEAD]
                q = rotate(u[:HEAD], cs, sn, 1.0).astype(bf16)
                qt[cc, j, :, here] = (q.astype(f32) * 0.125).astype(bf16)
                kt[j, cc, at, cols] = rotate(u[HEAD : 2 * HEAD], cs, sn, 1.0).astype(bf16)
                vt[j, cc, at, cols] = u[2 * HEAD :].astype(bf16)
        for cp in kvcopies(i):
            cp.start()
        for j in range(hc):
            both = jnp.concatenate([qt[0, j, :, here], qt[1, j, :, here]], axis=0)
            nat = both.astype(f32).T
            qn[0, j, here, :] = jnp.where(
                low_half, nat, jnp.where(lane == HEAD, 1.0, 0.0)
            ).astype(bf16)
            qn[1, j, here, :] = jnp.where(
                low_half, jnp.where(lane == 0, 1.0, 0.0), nat
            ).astype(bf16)
        return carry

    lax.fori_loop(0, NCH, qkv, 0)

    def kvwait(i, carry):
        for cp in kvcopies(i):
            cp.wait_recv()
        return carry

    lax.fori_loop(0, NCH, kvwait, 0)
    w_ox.wait_recv()
    w_oxc.start()
    for cp in locals_[NCH + 1 :]:
        cp.wait()
    for w in (w_o, w_oxc, w_g, w_u, w_d):
        w.wait_recv()

    def rows_of(i):
        return pl.ds(pl.multiple_of(i * tq, tq), tq)

    def hid_rows(cc, i):
        return pl.ds(pl.multiple_of(cc * ntok + i * tq, tq), tq)

    def own_of(i):
        return pl.ds(pl.multiple_of(i * cl, cl), cl)

    def ocopy(i):
        part = oall.at[x, rows_of(i)]
        return remote(part, part, oss.at[i], ors.at[i], xp)

    def mcopy(i):
        return remote(snd1.at[i], mrecv.at[i], mss.at[i], mrs.at[i], xp)

    def bcopy(i):
        return remote(dmb.at[i, x], dmb.at[i, x], bss.at[i], brs.at[i], xp)

    def dcopy(i):
        return remote(snd2.at[i], drecv.at[i], dss.at[i], drs.at[i], xp)

    def acopy(i):
        return remote(dab.at[i, x], dab.at[i, x], ass_.at[i], ars.at[i], xp)

    def ycopy(i):
        return pltpu.make_async_copy(ybuf.at[i], out_y.at[pl.ds(i * cl, cl)], ysem.at[i])

    def attend(i):
        rows = rows_of(i)
        for j in range(hc):
            outs = []
            for par in range(2):
                base = HEAD * (1 - par)
                qq = qn[par, j, rows, :]
                s = dot(qq, kt[j, par])
                top = jnp.max(s, axis=1, keepdims=True)
                p = jnp.exp(s - top).astype(bf16)
                oo = dot(p, vt[j, par], 1, 1)
                total = oo[:, base : base + 1]
                outs.append(oo * (1.0 / total))
                neg = -(top + jnp.log(total))
                hi = neg.astype(bf16).astype(f32)
                mid = (neg - hi).astype(bf16).astype(f32)
                lo = neg - hi - mid
                qf = qq.astype(f32)
                qf = jnp.where(lane == base + 1, hi, qf)
                qf = jnp.where(lane == base + 2, mid, qf)
                qf = jnp.where(lane == base + 3, lo, qf)
                qn[par, j, rows, :] = qf.astype(bf16)
            oall[x, rows, j * 2 * HEAD : (j + 1) * 2 * HEAD] = jnp.where(
                low_half, outs[0], outs[1]
            ).astype(bf16)
        ocopy(i).start()

    def mlp_fwd(i):
        rows, own = rows_of(i), own_of(i)
        ocopy(i).wait_recv()
        a = dot(oall[0, rows, :], wo[0].reshape(2 * qw, width))
        a += dot(oall[1, rows, :], wo[1].reshape(2 * qw, width))
        r = xall[i].reshape(tq, width).astype(f32) + a
        centre = r - mean(r)
        inv = lax.rsqrt(mean(centre * centre) + eps)
        n1 = centre * inv
        tmp[...] = n1.reshape(2, cl, width)
        n1own[own, :] = tmp[x]
        itmp[...] = jnp.broadcast_to(inv, (tq, 128)).reshape(2, cl, 128)
        inv1own[own, :] = itmp[x]
        x1 = n1 * ga[...]
        tmp[...] = x1.reshape(2, cl, width)
        rown[own, :] = tmp[x]
        xb = x1.astype(bf16)
        x1b[rows, :] = xb
        m = None
        for cc in range(2):
            g = dot(xb, wm[3 * cc])
            u = dot(xb, wm[3 * cc + 1])
            sg = 0.5 * jnp.tanh(0.5 * g) + 0.5
            si = g * sg
            hv = (si * u).astype(bf16)
            at = hid_rows(cc, i)
            act2[at, :] = si.astype(bf16)
            act1[at, :] = (u * (sg + si * (1.0 - sg))).astype(bf16)
            hid[at, :] = hv
            part = dot(hv, wm[3 * cc + 2])
            m = part if m is None else m + part
        mtmp[...] = m.reshape(2, cl, width)
        snd1[i] = mtmp[ox].astype(bf16)
        mcopy(i).start()

    def norm_two(i):
        own = own_of(i)
        mcopy(i).wait_recv()
        r = rown[own, :] + (mtmp[x] + mrecv[i].astype(f32))
        centre = r - mean(r)
        inv = lax.rsqrt(mean(centre * centre) + eps)
        n2 = centre * inv
        ybuf[i] = (n2 * gm[...]).astype(bf16)
        ycopy(i).start()
        dy = cotv[own, :].astype(f32)
        gbuf[1:2, :] += jnp.sum(dy * n2, axis=0, keepdims=True)
        e = dy * gm[...]
        dr = inv * (e - mean(e) - n2 * mean(e * n2))
        rown[own, :] = dr
        dmb[i, x] = dr.astype(bf16)
        bcopy(i).start()

    def mlp_bwd(i):
        bcopy(i).wait_recv()
        db = dmb[i].reshape(tq, width)
        d = None
        for cc in range(2):
            at = hid_rows(cc, i)
            dh = dot(db, wm[3 * cc + 2], 1, 1)
            dg = (dh * act1[at, :].astype(f32)).astype(bf16)
            du = (dh * act2[at, :].astype(f32)).astype(bf16)
            act1[at, :] = dg
            act2[at, :] = du
            part = dot(dg, wm[3 * cc], 1, 1) + dot(du, wm[3 * cc + 1], 1, 1)
            d = part if d is None else d + part
        dtmp[...] = d.reshape(2, cl, width)
        snd2[i] = dtmp[ox].astype(bf16)
        dcopy(i).start()

    def norm_one(i):
        own = own_of(i)
        dcopy(i).wait_recv()
        dx = rown[own, :] + (dtmp[x] + drecv[i].astype(f32))
        n1 = n1own[own, :]
        gbuf[0:1, :] += jnp.sum(dx * n1, axis=0, keepdims=True)
        e = dx * ga[...]
        dr = inv1own[own, 0:1] * (e - mean(e) - n1 * mean(e * n1))
        rown[own, :] = dr
        dab[i, x] = dr.astype(bf16)
        acopy(i).start()

    kb = min(1024, nkey)

    def attend_back(j, i):
        rows = rows_of(i)

        @when(j == 0)
        def _():
            acopy(i).wait_recv()

        @when(i == 0)
        def _():
            dkv[j % 2] = jnp.zeros(dkv.shape[1:], f32)

        da = dab[i].reshape(tq, width)
        cs = cos_t[:, rows]
        sn = sin_t[:, rows]
        lanes = pl.ds(pl.multiple_of(j * 2 * HEAD, 2 * HEAD), 2 * HEAD)
        dop = dot(da, wo[x, j].reshape(2 * HEAD, width), 1, 1).astype(bf16)
        dof = dop.astype(f32)
        prod = dof * oall[x, rows, lanes].astype(f32)
        dot_t = dof.T.astype(bf16)
        dqs = []
        for par in range(2):
            base = HEAD * (1 - par)
            mine = low_half if par == 0 else jnp.logical_not(low_half)
            neg = -jnp.sum(jnp.where(mine, prod, 0.0), axis=1, keepdims=True)
            hi = neg.astype(bf16).astype(f32)
            lo = neg - hi
            aug = jnp.where(lane == base, hi, jnp.where(lane == base + 1, lo, 0.0))
            doa = jnp.where(mine, dof, aug).astype(bf16)
            qq = qn[par, j, rows, :]
            dq = None
            for b in range(nkey // kb):
                kk = slice(b * kb, (b + 1) * kb)
                p = jnp.exp(dot(qq, kt[j, par, :, kk]))
                d = dot(doa, vt[j, par, :, kk])
                ds = (p * d).astype(bf16)
                pb = p.astype(bf16)
                dkv[j % 2, par, HEAD:, kk] += dot(dot_t[par * HEAD : (par + 1) * HEAD], pb)
                dkv[j % 2, par, :HEAD, kk] += dot(qt[par, j, :, rows], ds)
                part = dot(ds, kt[j, par, :, kk], 1, 1)
                dq = part if dq is None else dq + part
            dqs.append(dq)
        dqt = jnp.where(low_half, dqs[0], dqs[1]).T * 0.125
        at = pl.ds(pl.multiple_of(j * 3 * HEAD, HEAD), HEAD)
        for par in range(2):
            u = rotate(dqt[par * HEAD : (par + 1) * HEAD], cs, sn, -1.0)
            dpt[par, at, rows] = u.astype(bf16)

    stages = (attend, mlp_fwd, norm_two, mlp_bwd, norm_one)

    def step(t, carry):
        for lag in reversed(range(len(stages))):
            stage = stages[lag]

            @when(jnp.logical_and(t >= lag, t < NCH + lag))
            def _():
                stage(t - lag)

        return carry

    lax.fori_loop(0, NCH + 2, step, 0)

    blk = pl.ds(0, fq)
    blk2 = pl.ds(fq, fq)
    g_sent = (gsent, act1.at[blk], act1.at[blk2])

    def gcopy(n):
        return remote(g_sent[n], wm.at[3 + n], gss.at[n], grs.at[n], core)

    def gsum(n):
        gcopy(n).wait()
        wm[n] = (wm[n].astype(f32) + wm[3 + n].astype(f32)).astype(bf16)

    def give(n, dev):
        pl.semaphore_signal(credit.at[n], inc=1, device_id=dev, device_id_type=MESH)

    def half_of(ref, cc):
        return ref[pl.ds(pl.multiple_of(cc * ntok, ntok), ntok), :]

    def mlp_grads():
        norm_one(NCH - 2)
        mlp_bwd(NCH - 1)
        give(0, core)
        gsent[...] = dot(x1b[...], half_of(act1, oc), 0, 0).astype(bf16)
        wm[0] = dot(x1b[...], half_of(act1, c), 0, 0).astype(bf16)
        act1[blk, :] = dot(x1b[...], half_of(act2, oc), 0, 0).astype(bf16)
        pl.semaphore_wait(credit.at[0], 1)
        gcopy(0).start()
        gcopy(1).start()
        wm[1] = dot(x1b[...], half_of(act2, c), 0, 0).astype(bf16)
        dmball = dmb[...].reshape(ntok, width)
        act1[blk2, :] = dot(half_of(hid, oc), dmball, 0, 0).astype(bf16)
        gcopy(2).start()
        wm[2] = dot(half_of(hid, c), dmball, 0, 0).astype(bf16)
        give(1, core)
        for i in range(NCH):
            bcopy(i).wait_send()
        if ring:
            give(2, ydev)
            give(2, zdev)

            @when(inner)
            def _():
                give(2, mid)

        norm_one(NCH - 1)
        for n in range(3):
            gsum(n)
        pl.semaphore_wait(credit.at[1], 1)
        if ring:
            pl.semaphore_wait(credit.at[2], 2 + jnp.where(inner, 1, 0))

    place = jnp.where(y == 0, z, 7 - z)
    seg = fq // 16
    hops = 14

    def ring_row(p):
        p = (p + 8) % 8
        return {"rows": jnp.where(p < 4, 2 * p, 15 - 2 * p)}

    def ring_copies(u, k, to_slot):
        cps = []
        for d in range(2):
            sign = 1 - 2 * d
            at = d * 8 * seg + ((place - sign * k + 16) % 8) * seg
            rows = pl.ds(pl.multiple_of(at, 16), seg)
            if to_slot:
                slot = ((u * 2 + d) * 7 + k) * seg
                part = wm.at[u, rows]
                dst = act2.at[pl.ds(pl.multiple_of(slot, 16), seg)]
            else:
                part = dst = wm.at[3 + u, rows]
            cps.append(
                remote(part, dst, rss.at[u, d, k], rrs.at[u, d, k], ring_row(place + sign))
            )
        return cps

    def ring_step(m):
        u, k = m % 3, m // 3

        @when(k >= 1)
        def _():
            for cp in ring_copies(u, k - 1, False):
                cp.wait_recv()

        @when(jnp.logical_and(k >= 1, k <= 7))
        def _():
            for d in range(2):
                sign = 1 - 2 * d
                at = d * 8 * seg + ((place - sign * k + 16) % 8) * seg
                rows = pl.ds(pl.multiple_of(at, 16), seg)
                slot = pl.ds(pl.multiple_of(((u * 2 + d) * 7 + k - 1) * seg, 16), seg)
                wm[jnp.where(k == 7, 3 + u, u), rows, :] = (
                    wm[u, rows, :].astype(f32) + act2[slot, :].astype(f32)
                ).astype(bf16)

        @when(k <= 6)
        def _():
            for cp in ring_copies(u, k, True):
                cp.start()

        @when(jnp.logical_and(k >= 7, k < hops))
        def _():
            for cp in ring_copies(u, k, False):
                cp.start()

        @when(k >= 2)
        def _():
            for cp in ring_copies(u, k - 2, False):
                cp.wait_send()

    sub = 3 * HEAD

    def acore(b):
        src = hid.at[pl.ds(pl.multiple_of((4 + b) * sub, sub), sub)]
        dst = hid.at[pl.ds(pl.multiple_of(b * sub, sub), sub)]
        return remote(src, dst, gss.at[3 + b], grs.at[3 + b], core)

    def asum(b):
        acore(b).wait()
        got = hid[pl.ds(pl.multiple_of(b * sub, sub), sub), :]
        rows = pl.ds(pl.multiple_of(b * sub, sub), sub)
        agrad[rows, :] = (agrad[rows, :].astype(f32) + got.astype(f32)).astype(bf16)

    def astart(b, theirs, ours):
        hid[pl.ds(pl.multiple_of((4 + b) * sub, sub), sub), :] = theirs.astype(bf16)
        acore(b).start()
        agrad[pl.ds(pl.multiple_of(b * sub, sub), sub), :] = ours.astype(bf16)

    hs = sub // 2

    def tree(b, phase):
        mine = agrad.at[pl.ds(pl.multiple_of(b * sub + y * hs, hs), hs)]
        final = hid.at[pl.ds(pl.multiple_of(b * sub + y * hs, hs), hs)]
        buf_a = x1b.at[pl.ds(b * sub, hs)]
        buf_b = x1b.at[pl.ds(b * sub + hs, hs)]
        buf_c = dmb.at[b, 0, pl.ds(0, hs)]
        c0 = lambda: remote(agrad.at[pl.ds(pl.multiple_of(b * sub + (1 - y) * hs, hs), hs)], buf_a, fas.at[b, 0], far.at[b, 0], ydev)
        c1 = lambda: remote(mine, buf_b, fas.at[b, 1], far.at[b, 1], zdev)
        c2 = lambda: remote(mine, buf_c, fas.at[b, 2], far.at[b, 2], mid)
        c3 = lambda: remote(final, final, fas.at[b, 3], far.at[b, 3], zdev)
        c4 = lambda: remote(final, final, fas.at[b, 4], far.at[b, 4], ydev)

        def add(buf, dst):
            dst[...] = (mine[...].astype(f32) + buf[...].astype(f32)).astype(bf16)

        if phase == 0:
            c0().start()
        elif phase == 1:
            c0().wait_recv()
            add(buf_a, mine)

            @when(outer)
            def _():
                c1().start()
        elif phase == 2:

            @when(inner)
            def _():
                c1().wait_recv()
                add(buf_b, mine)
                c2().start()
        elif phase == 3:

            @when(inner)
            def _():
                c2().wait()
                add(buf_c, final)
                c3().start()
                c4().start()
        elif phase == 4:

            @when(outer)
            def _():
                c3().wait_recv()
                c4().start()
        else:
            c4().wait_recv()
            c0().wait_send()
            c4().wait_send()

            @when(outer)
            def _():
                c1().wait_send()

            @when(inner)
            def _():
                c3().wait_send()

    def gain_copy(n):
        return remote(gbuf, grecv.at[n], ns.at[n], nr.at[n], doubling[n])

    def gain_step(n):
        if n > 0:
            gain_copy(n - 1).wait()
            gbuf[...] += grecv[n - 1]
        if n < len(doubling):
            gain_copy(n).start()

    theirs_cols = pl.ds(pl.multiple_of(oc * ntok, ntok), ntok)
    mine_cols = pl.ds(pl.multiple_of(c * ntok, ntok), ntok)

    def kv_rows(j):
        return pl.ds(pl.multiple_of(j * 3 * HEAD + HEAD, HEAD), 2 * HEAD)

    def kvback(j):
        return remote(dpt.at[:, kv_rows(j)], dkvr.at[j], css.at[j], crs.at[j], core)

    def kv_send(j):
        dpt[:, kv_rows(j), :] = dkv[j % 2, :, :, theirs_cols].astype(bf16)
        kvback(j).start()

    def kv_finish(j):
        kvback(j).wait()
        base = j * 3 * HEAD
        for par in range(2):
            u = dkv[j % 2, par, :, mine_cols] + dkvr[j, par].astype(f32)
            dk = rotate(u[:HEAD], cos_t[...], sin_t[...], -1.0)
            dpt[par, pl.ds(pl.multiple_of(base + HEAD, HEAD), HEAD), :] = dk.astype(bf16)
            dpt[par, pl.ds(pl.multiple_of(base + 2 * HEAD, HEAD), HEAD), :] = u[HEAD:].astype(bf16)

    def qkv_grads(j):
        rows = pl.ds(pl.multiple_of(j * sub, HEAD), sub)
        xr = xall[...].reshape(ntok, width)
        astart(1 + j, dot(dpt[oc, rows, :], xr), dot(dpt[c, rows, :], xr))

    def out_grads():
        both = dot(oall[x], dab[...].reshape(ntok, width), 0, 0).reshape(hc, 2, HEAD, width)
        first = both[:, 0].reshape(sub, width)
        second = both[:, 1].reshape(sub, width)
        astart(0, jnp.where(c == 0, second, first), jnp.where(c == 0, first, second))

    def at_step(q, n):
        return when(q == n)

    def back(q, carry):
        j, i = q // NCH, q % NCH
        attend_back(j, i)

        @at_step(q, 0)
        def _():
            mlp_grads()

        @when(i == NCH - 1)
        def _():
            @when(j < hc - 1)
            def _():
                kv_send(j)

        @when(jnp.logical_and(i == 0, j > 0))
        def _():
            kv_finish(j - 1)
            qkv_grads(j - 1)

        @at_step(q, 3)
        def _():
            out_grads()

        @at_step(q, 4)
        def _():
            asum(0)

        @when(jnp.logical_and(i == 1, j > 0))
        def _():
            asum(j)

        for n in range(len(doubling) + 1):

            @at_step(q, min(2 + n, NCH * hc - 1))
            def _():
                gain_step(n)

        if ring:
            for b, ph, n in TREE_PLAN:

                @at_step(q, n)
                def _():
                    tree(b, ph)

            for extra in range(2):
                ring_step(2 * q + extra)
        return carry

    lax.fori_loop(0, NCH * hc, back, 0)

    def fcopy(i):
        return remote(snd1.at[i], mrecv.at[i], fss.at[i], frs.at[i], xp)

    def input_terms(i, who):
        cols = pl.ds(pl.multiple_of(i * tq + who * cl, cl), cl)
        d = None
        for cc in range(2):
            part = dot(dpt[cc, :, cols], wqt[cc], 0, 0)
            d = part if d is None else d + part
        return d

    def rings(first, last):
        if ring:

            def one(m, carry):
                ring_step(m)
                return carry

            lax.fori_loop(first, last, one, 0)

    def trees(*steps):
        if ring:
            for b, ph in steps:
                tree(b, ph)

    last = hc - 1
    done = 2 * NCH * hc
    kv_send(last)
    trees((2, 2), (0, 5), (1, 4))
    rings(done, done + 2)
    kv_finish(last)
    for i in range(NCH):
        mcopy(i).wait_send()
        snd1[i] = input_terms(i, ox).astype(bf16)
        fcopy(i).start()
    qkv_grads(last)
    rings(done + 2, done + 4)
    asum(1 + last)
    trees((3, 0), (2, 3), (1, 5))
    rings(done + 4, done + 7)
    trees((3, 1), (2, 4))
    rings(done + 7, done + 10)
    trees((3, 2), (2, 5))
    rings(done + 10, done + 13)
    trees((3, 3))
    rings(done + 13, done + 16)
    trees((3, 4))

    for i in range(NCH):
        d = input_terms(i, x)
        fcopy(i).wait_recv()
        own = pl.ds(i * cl, cl)
        d = rown[own, :] + (d + mrecv[i].astype(f32))
        ycopy(i).wait()
        ybuf[i] = d.astype(bf16)
        pltpu.make_async_copy(ybuf.at[i], out_dx.at[own], lsem.at[i]).start()
    rings(done + 16, 3 * (hops + 1))
    trees((3, 5))

    def result_copies():
        return [
            pltpu.make_async_copy(wm.at[pl.ds(3 if ring else 0, 3)], g_mlp, gls.at[0]),
            pltpu.make_async_copy(
                hid.at[pl.ds(0, (1 + hc) * sub)] if ring else agrad, g_att, gls.at[1]
            ),
        ]

    for cp in result_copies():
        cp.start()
    g_gain[...] = gbuf[...]

    for i in range(NCH):
        own = pl.ds(i * cl, cl)
        pltpu.make_async_copy(ybuf.at[i], out_dx.at[own], lsem.at[i]).wait()
        xcopy(i).wait_send()
        for cp in kvcopies(i):
            cp.wait_send()
        ocopy(i).wait_send()
        dcopy(i).wait_send()
        acopy(i).wait_send()
        fcopy(i).wait_send()
    for w in (w_q, w_o, w_ox, w_oxc, w_g, w_u, w_d):
        w.wait_send()
    if ring:
        for u in range(3):
            for cp in ring_copies(u, hops - 1, False):
                cp.wait_send()
    for cp in result_copies():
        cp.wait()


TREE_PLAN = (
    (0, 0, 4), (0, 1, 6), (0, 2, 8), (0, 3, 10), (0, 4, 11),
    (1, 0, 5), (1, 1, 7), (1, 2, 9), (1, 3, 11),
    (2, 0, 9), (2, 1, 11),
)


def on_device(
    nrows, tokens, lengths, w_qkv, w_out, w_gate, w_up, w_down, gain_attn, gain_mlp, cotangent
):
    _, length, width = tokens.shape
    qw = w_qkv.shape[2]
    fq = w_gate.shape[1]
    hc = qw // HEAD
    nh = 2 * hc
    cl = length // NCH
    tq = 2 * cl
    ntok = 2 * length
    nkey = 2 * ntok
    h = lax.axis_index("heads")
    c = h % 2

    order = jnp.arange(nkey, dtype=jnp.int32).reshape(2, NCH, 2, cl)
    cores = lax.broadcasted_iota(jnp.int32, order.shape, 0)
    chunk = lax.broadcasted_iota(jnp.int32, order.shape, 1)
    xs = lax.broadcasted_iota(jnp.int32, order.shape, 2)
    place = lax.broadcasted_iota(jnp.int32, order.shape, 3)
    position = (2 * xs + cores) * length + chunk * cl + place
    valid = position.reshape(1, nkey) < lengths[0]
    row = lax.broadcasted_iota(jnp.int32, (HEAD, nkey), 0)
    augk = jnp.where(
        row == 0, jnp.where(valid, 0.0, -1e30), jnp.where(row < 4, 1.0, 0.0)
    ).astype(bf16)
    here = ((2 * xs[0] + c) * length + chunk[0] * cl + place[0]).reshape(1, ntok).astype(f32)
    half = HEAD // 2
    freqs = rope_base ** (-jnp.arange(half).astype(f32) / half)
    angles = freqs[:, None] * here
    cos_t, sin_t = jnp.cos(angles), jnp.sin(angles)

    wqt = w_qkv.reshape(3, width, hc, HEAD).transpose(2, 0, 3, 1).reshape(3 * qw, width)

    hbm = pl.BlockSpec(memory_space=pl.ANY)
    vmem = pl.BlockSpec(memory_space=pltpu.VMEM)
    S = jax.ShapeDtypeStruct
    V = pltpu.VMEM
    dma = pltpu.SemaphoreType.DMA
    doublings = 2 + (nrows - 1).bit_length()
    scratch = [
        V((NCH, 2, cl, width), bf16),
        V((length, width), bf16),
        V((2, 3 * qw, width), bf16),
        V((2, hc, 2, HEAD, width), bf16),
        V((6, width, fq), bf16),
        V((hc, 2, 2 * HEAD, nkey), bf16),
        V((hc, 2, 2 * HEAD, nkey), bf16),
        V((2, hc, ntok, 2 * HEAD), bf16),
        V((2, hc, HEAD, ntok), bf16),
        V((2, ntok, 2 * qw), bf16),
        V((ntok, width), bf16),
        V((length, width), f32),
        V((length, width), f32),
        V((length, 128), f32),
        V((2 * ntok, fq), bf16),
        V((2 * ntok, fq), bf16),
        V((2 * ntok, fq), bf16),
        V((NCH, 2, cl, width), bf16),
        V((NCH, 2, cl, width), bf16),
        V((NCH, cl, width), bf16),
        V((NCH, cl, width), bf16),
        V((NCH, cl, width), bf16),
        V((NCH, cl, width), bf16),
        V((2, cl, width), f32),
        V((2, cl, width), f32),
        V((2, cl, width), f32),
        V((2, cl, 128), f32),
        V((2, 2, 2 * HEAD, nkey), f32),
        V((hc, 2, 2 * HEAD, ntok), bf16),
        V((2, 3 * qw, ntok), bf16),
        V((NCH, cl, width), bf16),
        V((width, fq), bf16),
        V(((1 + hc) * 3 * HEAD, width), bf16),
        V((8, width), f32),
        V((doublings, 8, width), f32),
        dma((NCH + 6,)),
        dma((7,)), dma((7,)),
        dma((NCH,)), dma((NCH,)),
        dma((NCH, 4)), dma((NCH, 4)),
        dma((NCH,)), dma((NCH,)),
        dma((NCH,)), dma((NCH,)),
        dma((NCH,)), dma((NCH,)),
        dma((NCH,)), dma((NCH,)),
        dma((NCH,)), dma((NCH,)),
        dma((hc,)), dma((hc,)),
        dma((NCH,)), dma((NCH,)),
        dma((4 + hc,)), dma((4 + hc,)), dma((2,)),
        dma((3, 2, 14)), dma((3, 2, 14)),
        dma((1 + hc, 5)), dma((1 + hc, 5)),
        dma((doublings,)), dma((doublings,)),
        dma((NCH,)),
        pltpu.SemaphoreType.REGULAR((3,)),
    ]
    outs = pl.pallas_call(
        functools.partial(layer_kernel, nrows),
        out_shape=[
            S((length, width), bf16), S((length, width), bf16),
            S((3, width, fq), bf16), S(((1 + hc) * 3 * HEAD, width), bf16), S((8, width), f32),
        ],
        in_specs=[hbm] * 7 + [vmem] * 5,
        out_specs=[hbm] * 4 + [vmem],
        scratch_shapes=scratch,
        compiler_params=pltpu.CompilerParams(
            collective_id=0, has_side_effects=True, vmem_limit_bytes=VLIM
        ),
    )(
        tokens[0], cotangent[0], wqt, w_out.reshape(hc, HEAD, width), w_gate, w_up, w_down,
        gain_attn[None], gain_mlp[None], cos_t, sin_t, augk,
    )
    y, dx, g_mlp, g_att, g_gain = outs
    if nrows != 8:
        g_mlp, g_att = lax.psum((g_mlp, g_att), "rows")
    g_att = g_att.reshape(1 + hc, 3 * HEAD, width)
    grad_qkv = g_att[1:].reshape(hc, 3, HEAD, width).transpose(1, 3, 0, 2)
    return (
        y[None], dx[None], grad_qkv.astype(f32).reshape(3, width, qw), g_att[0].astype(f32),
        g_mlp[0].astype(f32), g_mlp[1].astype(f32), g_mlp[2].astype(f32), g_gain[0], g_gain[1],
    )


VLIM = 64 * 2**20


def solution(mesh):
    in_specs = (
        P("rows", "heads", None),
        P("rows"),
        P(None, None, "heads"),
        P("heads", None),
        P(None, "heads"),
        P(None, "heads"),
        P("heads", None),
        P(),
        P(),
        P("rows", "heads", None),
    )
    out_specs = (
        P("rows", "heads", None),
        P("rows", "heads", None),
        P(None, None, "heads"),
        P("heads", None),
        P(None, "heads"),
        P(None, "heads"),
        P("heads", None),
        P(),
        P(),
    )
    return jax.shard_map(
        functools.partial(on_device, mesh.shape["rows"]), mesh=mesh, in_specs=in_specs, out_specs=out_specs, check_vma=False
    )
```

time: 382 us -> 255 us (0.67)
  waiting for transfers between devices: 129 us -> 0 us
  Pallas kernels: 180 us -> 237 us
  blocking collectives: 42.3 us -> 0 us
  between operations: 14.8 us -> 1.41 us
    psum x1 -> x0, waiting for transfers between devices: 129 us -> none  [on_device(): gqt, go, gg, gu, gd = lax.psum((gqt, go, gg, gu, gd), 'rows')]
    pallas_call x1, Pallas kernels: 180 us -> 237 us  [on_device(): pl.pallas_call(functools.partial(layer_kernel, nrows), out_shape=[S((leng...]
    psum x1 -> x0, blocking collectives: 42.3 us -> none  [on_device(): gga, ggm = lax.psum((gga, ggm), ('rows', 'heads'))]
  transfers between devices with their start and end apart: 1 -> 0, of which waited for: 1 -> 0; matrix products, arithmetic and copies ran while one was open for 0% -> 0% of each run, Pallas kernels for 0% -> 0%
where the time goes in v2:
time: 255 us; the launch traced here: 254 us
  Pallas kernels  237 us (93%)
  other arithmetic  8.37 us (3%)
  local copies, waits for them, and re-layouts  7.89 us (3%)
    pallas_call x1, Pallas kernels, on_device(): pl.pallas_call(functools.partial(layer_kernel, nrows), out_shape=[S((leng...  237 us
    convert_element_type x1, other arithmetic, on_device(): g_mlp[2].astype(f32)  5.21 us

profile of v2, /device:TPU:0, one launch (start us, length us, event | category | flops | bytes accessed | tf_op | source)
XLA Modules:
  0.0 254.3 jit_solution(6940229235770092857)
XLA Ops:
  0.6 0.0 copy-start.3
  0.7 0.0 copy-start.4
  0.7 1.2 multiply_sine_fusion
  2.0 2.1 copy.19
  4.8 0.1 compare_select_fusion
  4.9 0.8 select_convert_fusion.augk
  5.7 0.0 copy-done.3
  5.7 0.6 broadcast_in_dim.37.ga
  6.3 0.0 copy-done.4
  6.3 0.6 broadcast_in_dim.38.gm
  6.8 236.6 %shard_map.169 = (bf16[512,768]{1,0:T(8,128)(2,1)}, bf16[512,768]{1,0:T(8,128)(2,1)}, bf16[3,768,768]{2,1,0:T(8,128)(2,1)}, bf16[768,768]{1,0:T(8,128)(2,1)}, f32[8,768]{1,0:T(8,128)}) custom-call(bf16[512,768]{1,0:T(8,128)(2,1)} %bitcast.34, bf16[512,768]{1,0:T(8,128)(2,1)} %bitcast.35, bf16[576,768]{1,0:T(8,128)(2,1)} %bitcast.29, ...), custom_call_target="tpu_custom_call" | custom-call | tf_op jit(solution)/shard_map/pallas_call | solution.py:875
  243.5 0.0 copy-start
  243.5 5.2 %bitcast_convert_fusion = (f32[768,768]{1,0:T(8,128)}, f32[768,768]{1,0:T(8,128)}, f32[768,768]{1,0:T(8,128)}) fusion(bf16[3,768,768]{2,1,0:T(8,128)(2,1)} %get-tuple-element.17), kind=kLoop, calls=%fused_computation.1 | loop fusion | flops 1769472 | bytes 10616832 | tf_op jit(solution)/shard_map/convert_element_type | solution.py:898
  248.7 0.0 copy-done
  248.7 0.1 slice.29
  248.8 0.2 convert_bitcast_fusion
  248.9 0.0 copy-start.2
  249.0 1.3 copy.20
  250.3 0.0 copy-start.1
  250.3 0.9 slice_convert_fusion
  251.1 1.4 slice_reduce_fusion
  252.6 0.0 copy-done.2
  252.6 0.9 copy.24
  253.4 0.0 copy-done.1
  253.4 0.9 copy.25
  (8 shorter events, 0.0 us)
Async XLA Ops:
  0.6 5.0 %copy-start.3 = (f32[768]{0:T(1024)S(1)}, f32[768]{0:T(1024)}, u32[]{:S(2)}) copy-start(f32[768]{0:T(1024)} %param.17) | copy-start | bytes 9220
  0.7 5.6 %copy-start.4 = (f32[768]{0:T(1024)S(1)}, f32[768]{0:T(1024)}, u32[]{:S(2)}) copy-start(f32[768]{0:T(1024)} %param.18) | copy-start | bytes 9220
  243.5 5.2 %copy-start = (bf16[768,768]{1,0:T(8,128)(2,1)S(1)}, bf16[768,768]{1,0:T(8,128)(2,1)}, u32[]{:S(2)}) copy-start(bf16[768,768]{1,0:T(8,128)(2,1)} %get-tuple-element.16) | copy-start | bytes 3538948
  248.9 3.6 %copy-start.2 = (bf16[512,768]{1,0:T(8,128)(2,1)S(1)}, bf16[512,768]{1,0:T(8,128)(2,1)}, u32[]{:S(2)}) copy-start(bf16[512,768]{1,0:T(8,128)(2,1)} %get-tuple-element.14) | copy-start | bytes 2359300
  250.3 3.2 %copy-start.1 = (bf16[512,768]{1,0:T(8,128)(2,1)S(1)}, bf16[512,768]{1,0:T(8,128)(2,1)}, u32[]{:S(2)}) copy-start(bf16[512,768]{1,0:T(8,128)(2,1)} %get-tuple-element.15) | copy-start | bytes 2359300

commit v3 on v2

--- a/solution.py
+++ b/solution.py
@@ -2,6 +2,7 @@
 
 import jax
 import jax.numpy as jnp
+import numpy as np
 from jax import lax
 from jax.experimental import pallas as pl
 from jax.experimental.pallas import tpu as pltpu
@@ -25,12 +26,12 @@
 
 
 def layer_kernel(
-    nrows, tok, cot, wqt_in, wo_in, wg_in, wu_in, wd_in, ga, gm, cos_t, sin_t, augk,
-    out_y, out_dx, g_mlp, g_att, g_gain,
+    nrows, tok, cot, wq_in, wo_in, wg_in, wu_in, wd_in, turns, lengths, ga_in, gm_in, place_in,
+    out_y, out_dx, g_mlp, g_out, g_qkv, g_ga, g_gm,
     xall, cotv, wqt, wo, wm, kt, vt, qn, qt, oall, x1b, rown, n1own, inv1own,
-    act1, act2, hid, dmb, dab, mrecv, drecv, snd1, snd2, tmp, mtmp, dtmp, itmp,
-    dkv, dkvr, dpt, ybuf, gsent, agrad, gbuf, grecv,
-    lsem, wss, wrs, xss, xrs, kss, krs, oss, ors, mss, mrs, bss, brs, dss, drs, ass_, ars,
+    act1, act2, hid, dmb, dab, mrecv, drecv, snd1, snd2, tmp, itmp,
+    dkv, dkvr, dpt, ybuf, agrad, gbuf, grecv, turn,
+    lsem, wqs, wqr, wss, wrs, xss, xrs, kss, krs, oss, ors, mss, mrs, bss, brs, dss, drs, ass_, ars,
     css, crs, fss, frs, gss, grs, gls, rss, rrs, fas, far, ns, nr, ysem, credit,
 ):
     ring = nrows == 8
@@ -90,7 +91,8 @@
             cps.append(pltpu.make_async_copy(tok.at[pl.ds(i * cl, cl)], xall.at[i, x], lsem.at[i]))
         n = NCH
         for src, dst in (
-            (wqt_in, wqt.at[c]), (wo_in, wo.at[x, :, c]), (wg_in, wm.at[3 * c]),
+            (wq_in.at[0], wqt.at[c, :, 0]), (wq_in.at[1], wqt.at[c, :, 1]),
+            (wq_in.at[2], wqt.at[c, :, 2]), (turns.at[c], turn), (wo_in, wo.at[x, :, c]), (wg_in, wm.at[3 * c]),
             (wu_in, wm.at[3 * c + 1]), (wd_in, wm.at[3 * c + 2]), (cot, cotv),
         ):
             cps.append(pltpu.make_async_copy(src, dst, lsem.at[n]))
@@ -106,14 +108,17 @@
     def xcopy(i):
         return remote(tok.at[pl.ds(i * cl, cl)], xall.at[i, x], xss.at[i], xrs.at[i], xp)
 
-    w_q = remote(wqt_in, wqt.at[c], wss.at[0], wrs.at[0], core)
+    w_q = [
+        remote(wq_in.at[n], wqt.at[c, :, n], wqs.at[n], wqr.at[n], core) for n in range(3)
+    ]
     w_o = remote(wo_in, wo.at[x, :, c], wss.at[1], wrs.at[1], core)
     w_ox = remote(wo_in, wo.at[x, :, c], wss.at[2], wrs.at[2], xp)
     w_oxc = remote(wo.at[ox, :, c], wo.at[ox, :, c], wss.at[3], wrs.at[3], core)
     w_g = remote(wg_in, wm.at[3 * c], wss.at[4], wrs.at[4], core)
     w_u = remote(wu_in, wm.at[3 * c + 1], wss.at[5], wrs.at[5], core)
     w_d = remote(wd_in, wm.at[3 * c + 2], wss.at[6], wrs.at[6], core)
-    w_q.start()
+    for w in w_q:
+        w.start()
     for i in range(NCH):
         xcopy(i).start()
     w_o.start()
@@ -124,9 +129,16 @@
 
     nrow = lax.broadcasted_iota(jnp.int32, (HEAD, nkey), 0)
     vrows = jnp.where(nrow < 2, 1.0, 0.0).astype(bf16)
+    valid = place_in[...] < lengths[0]
+    augk = jnp.where(
+        nrow == 0, jnp.where(valid, 0.0, -1e30), jnp.where(nrow < 4, 1.0, 0.0)
+    ).astype(bf16)
+    ga = ga_in[...].reshape(1, width)
+    gm = gm_in[...].reshape(1, width)
+    cos_t, sin_t = turn.at[0], turn.at[1]
     for pr in range(hc):
-        kt[pr, 0, HEAD:, :] = augk[...]
-        kt[pr, 1, :HEAD, :] = augk[...]
+        kt[pr, 0, HEAD:, :] = augk
+        kt[pr, 1, :HEAD, :] = augk
         vt[pr, 0, HEAD:, :] = vrows
         vt[pr, 1, :HEAD, :] = vrows
     gbuf[...] = jnp.zeros_like(gbuf)
@@ -150,8 +162,10 @@
                 n += 1
         return cps
 
-    locals_[NCH].wait()
-    w_q.wait_recv()
+    for cp in locals_[NCH : NCH + 4]:
+        cp.wait()
+    for w in w_q:
+        w.wait_recv()
 
     def qkv(i, carry):
         pltpu.make_async_copy(tok.at[pl.ds(i * cl, cl)], xall.at[i, x], lsem.at[i]).wait()
@@ -162,7 +176,7 @@
         cs = cos_t[:, here]
         sn = sin_t[:, here]
         for cc in range(2):
-            pt = dot(wqt[cc], xb, 1, 1)
+            pt = dot(wqt[cc].reshape(3 * qw, width), xb, 1, 1)
             at = slice(cc * HEAD, cc * HEAD + HEAD)
             for j in range(hc):
                 u = pt[j * 3 * HEAD : (j + 1) * 3 * HEAD]
@@ -193,7 +207,7 @@
     lax.fori_loop(0, NCH, kvwait, 0)
     w_ox.wait_recv()
     w_oxc.start()
-    for cp in locals_[NCH + 1 :]:
+    for cp in locals_[NCH + 4 :]:
         cp.wait()
     for w in (w_o, w_oxc, w_g, w_u, w_d):
         w.wait_recv()
@@ -224,7 +238,7 @@
         return remote(dab.at[i, x], dab.at[i, x], ass_.at[i], ars.at[i], xp)
 
     def ycopy(i):
-        return pltpu.make_async_copy(ybuf.at[i], out_y.at[pl.ds(i * cl, cl)], ysem.at[i])
+        return pltpu.make_async_copy(ybuf.at[i], out_y.at[own_of(i)], ysem.at[i])
 
     def attend(i):
         rows = rows_of(i)
@@ -266,9 +280,7 @@
         n1own[own, :] = tmp[x]
         itmp[...] = jnp.broadcast_to(inv, (tq, 128)).reshape(2, cl, 128)
         inv1own[own, :] = itmp[x]
-        x1 = n1 * ga[...]
-        tmp[...] = x1.reshape(2, cl, width)
-        rown[own, :] = tmp[x]
+        x1 = n1 * ga
         xb = x1.astype(bf16)
         x1b[rows, :] = xb
         m = None
@@ -284,22 +296,24 @@
             hid[at, :] = hv
             part = dot(hv, wm[3 * cc + 2])
             m = part if m is None else m + part
-        mtmp[...] = m.reshape(2, cl, width)
-        snd1[i] = mtmp[ox].astype(bf16)
+        tmp[...] = m.reshape(2, cl, width)
+        snd1[i] = tmp[ox].astype(bf16)
         mcopy(i).start()
+        tmp[...] = (x1 + m).reshape(2, cl, width)
+        rown[own, :] = tmp[x]
 
     def norm_two(i):
         own = own_of(i)
         mcopy(i).wait_recv()
-        r = rown[own, :] + (mtmp[x] + mrecv[i].astype(f32))
+        r = rown[own, :] + mrecv[i].astype(f32)
         centre = r - mean(r)
         inv = lax.rsqrt(mean(centre * centre) + eps)
         n2 = centre * inv
-        ybuf[i] = (n2 * gm[...]).astype(bf16)
+        ybuf[i] = (n2 * gm).astype(bf16)
         ycopy(i).start()
         dy = cotv[own, :].astype(f32)
         gbuf[1:2, :] += jnp.sum(dy * n2, axis=0, keepdims=True)
-        e = dy * gm[...]
+        e = dy * gm
         dr = inv * (e - mean(e) - n2 * mean(e * n2))
         rown[own, :] = dr
         dmb[i, x] = dr.astype(bf16)
@@ -318,17 +332,18 @@
             act2[at, :] = du
             part = dot(dg, wm[3 * cc], 1, 1) + dot(du, wm[3 * cc + 1], 1, 1)
             d = part if d is None else d + part
-        dtmp[...] = d.reshape(2, cl, width)
-        snd2[i] = dtmp[ox].astype(bf16)
-        dcopy(i).start()
+        tmp[...] = d.reshape(2, cl, width)
+        snd2[i] = tmp[ox].astype(bf16)
+        own = own_of(i)
+        rown[own, :] = rown[own, :] + tmp[x]
 
     def norm_one(i):
         own = own_of(i)
         dcopy(i).wait_recv()
-        dx = rown[own, :] + (dtmp[x] + drecv[i].astype(f32))
+        dx = rown[own, :] + drecv[i].astype(f32)
         n1 = n1own[own, :]
         gbuf[0:1, :] += jnp.sum(dx * n1, axis=0, keepdims=True)
-        e = dx * ga[...]
+        e = dx * ga
         dr = inv1own[own, 0:1] * (e - mean(e) - n1 * mean(e * n1))
         rown[own, :] = dr
         dab[i, x] = dr.astype(bf16)
@@ -383,69 +398,83 @@
             u = rotate(dqt[par * HEAD : (par + 1) * HEAD], cs, sn, -1.0)
             dpt[par, at, rows] = u.astype(bf16)
 
-    stages = (attend, mlp_fwd, norm_two, mlp_bwd, norm_one)
-
-    def step(t, carry):
-        for lag in reversed(range(len(stages))):
-            stage = stages[lag]
-
-            @when(jnp.logical_and(t >= lag, t < NCH + lag))
-            def _():
-                stage(t - lag)
-
-        return carry
-
-    lax.fori_loop(0, NCH + 2, step, 0)
-
-    blk = pl.ds(0, fq)
-    blk2 = pl.ds(fq, fq)
-    g_sent = (gsent, act1.at[blk], act1.at[blk2])
+    g_own = (0, 1, 6)
+    g_got = (3, 4, 7)
+    g_sent = (2, 5, 8)
 
     def gcopy(n):
-        return remote(g_sent[n], wm.at[3 + n], gss.at[n], grs.at[n], core)
-
-    def gsum(n):
-        gcopy(n).wait()
-        wm[n] = (wm[n].astype(f32) + wm[3 + n].astype(f32)).astype(bf16)
+        return remote(wm.at[g_sent[n]], wm.at[g_got[n]], gss.at[n], grs.at[n], core)
 
     def give(n, dev):
         pl.semaphore_signal(credit.at[n], inc=1, device_id=dev, device_id_type=MESH)
 
-    def half_of(ref, cc):
-        return ref[pl.ds(pl.multiple_of(cc * ntok, ntok), ntok), :]
-
-    def mlp_grads():
-        norm_one(NCH - 2)
-        mlp_bwd(NCH - 1)
-        give(0, core)
-        gsent[...] = dot(x1b[...], half_of(act1, oc), 0, 0).astype(bf16)
-        wm[0] = dot(x1b[...], half_of(act1, c), 0, 0).astype(bf16)
-        act1[blk, :] = dot(x1b[...], half_of(act2, oc), 0, 0).astype(bf16)
-        pl.semaphore_wait(credit.at[0], 1)
-        gcopy(0).start()
-        gcopy(1).start()
-        wm[1] = dot(x1b[...], half_of(act2, c), 0, 0).astype(bf16)
-        dmball = dmb[...].reshape(ntok, width)
-        act1[blk2, :] = dot(half_of(hid, oc), dmball, 0, 0).astype(bf16)
-        gcopy(2).start()
-        wm[2] = dot(half_of(hid, c), dmball, 0, 0).astype(bf16)
-        give(1, core)
-        for i in range(NCH):
-            bcopy(i).wait_send()
-        if ring:
-            give(2, ydev)
+    def tall(ref, cc):
+        return ref.at[pl.ds(pl.multiple_of(cc * ntok, ntok), ntok)]
+
+    def grad_into(dst, left, right):
+        tile = min(256, width)
+
+        def one(n, carry):
+            at = pl.ds(pl.multiple_of(n * tile, tile), tile)
+            dst[at, :] = dot(left[:, at], right[...].reshape(ntok, width), 0, 0).astype(bf16)
+            return carry
+
+        lax.fori_loop(0, width // tile, one, 0)
+
+    def grad(n):
+        left = (x1b, x1b, hid)[n]
+        right = (act1, act2, dmb)[n]
+        if n < 2:
+            grad_into(wm.at[g_sent[n]], left, tall(right, oc))
+            grad_into(wm.at[g_own[n]], left, tall(right, c))
+            if n == 0:
+                pl.semaphore_wait(credit.at[0], 1)
+            gcopy(n).start()
+        else:
+            grad_into(wm.at[g_sent[n]], tall(left, oc), right)
+            gcopy(n).start()
+            grad_into(wm.at[g_own[n]], tall(left, c), right)
+        if n == 2 and ring:
             give(2, zdev)
+
+            @when(outer)
+            def _():
+                give(2, ydev)
 
             @when(inner)
             def _():
                 give(2, mid)
 
-        norm_one(NCH - 1)
-        for n in range(3):
-            gsum(n)
+        if n == 1:
+            give(1, core)
+
+            def sent(i, carry):
+                bcopy(i).wait_send()
+                return carry
+
+            lax.fori_loop(0, NCH, sent, 0)
+            if ring:
+                give(3, ydev)
+                give(3, zdev)
+
+                @when(inner)
+                def _():
+                    give(3, mid)
+
+    def gsum(n):
+        gcopy(n).wait()
+        own, got = g_own[n], g_got[n]
+        wm[own] = (wm[own].astype(f32) + wm[got].astype(f32)).astype(bf16)
+        if n == 2 and ring:
+            pl.semaphore_wait(credit.at[2], 2)
+
+    def weights_free():
+        give(0, core)
+
+    def buffers_free():
         pl.semaphore_wait(credit.at[1], 1)
         if ring:
-            pl.semaphore_wait(credit.at[2], 2 + jnp.where(inner, 1, 0))
+            pl.semaphore_wait(credit.at[3], 2 + jnp.where(inner, 1, 0))
 
     place = jnp.where(y == 0, z, 7 - z)
     seg = fq // 16
@@ -463,19 +492,27 @@
             rows = pl.ds(pl.multiple_of(at, 16), seg)
             if to_slot:
                 slot = ((u * 2 + d) * 7 + k) * seg
-                part = wm.at[u, rows]
-                dst = act2.at[pl.ds(pl.multiple_of(slot, 16), seg)]
+                part = wm.at[ring_own(u), rows]
+                dst = hid.at[pl.ds(pl.multiple_of(slot, 16), seg)]
             else:
-                part = dst = wm.at[3 + u, rows]
+                part = dst = wm.at[ring_final(u), rows]
             cps.append(
                 remote(part, dst, rss.at[u, d, k], rrs.at[u, d, k], ring_row(place + sign))
             )
         return cps
 
+    def ring_own(u):
+        return jnp.where(u == 0, 6, u - 1)
+
+    def ring_final(u):
+        return jnp.where(u == 0, 7, u + 2)
+
     def ring_step(m):
-        u, k = m % 3, m // 3
-
-        @when(k >= 1)
+        u = m % 3
+        k = m // 3 - RING_LAG * u
+        live = jnp.logical_and(k >= 0, k <= hops)
+
+        @when(jnp.logical_and(live, k >= 1))
         def _():
             for cp in ring_copies(u, k - 1, False):
                 cp.wait_recv()
@@ -487,11 +524,12 @@
                 at = d * 8 * seg + ((place - sign * k + 16) % 8) * seg
                 rows = pl.ds(pl.multiple_of(at, 16), seg)
                 slot = pl.ds(pl.multiple_of(((u * 2 + d) * 7 + k - 1) * seg, 16), seg)
-                wm[jnp.where(k == 7, 3 + u, u), rows, :] = (
-                    wm[u, rows, :].astype(f32) + act2[slot, :].astype(f32)
+                src = ring_own(u)
+                wm[jnp.where(k == 7, ring_final(u), src), rows, :] = (
+                    wm[src, rows, :].astype(f32) + hid[slot, :].astype(f32)
                 ).astype(bf16)
 
-        @when(k <= 6)
+        @when(jnp.logical_and(live, k <= 6))
         def _():
             for cp in ring_copies(u, k, True):
                 cp.start()
@@ -501,7 +539,7 @@
             for cp in ring_copies(u, k, False):
                 cp.start()
 
-        @when(k >= 2)
+        @when(jnp.logical_and(live, k >= 2))
         def _():
             for cp in ring_copies(u, k - 2, False):
                 cp.wait_send()
@@ -509,18 +547,18 @@
     sub = 3 * HEAD
 
     def acore(b):
-        src = hid.at[pl.ds(pl.multiple_of((4 + b) * sub, sub), sub)]
-        dst = hid.at[pl.ds(pl.multiple_of(b * sub, sub), sub)]
+        src = act2.at[pl.ds(pl.multiple_of((4 + b) * sub, sub), sub)]
+        dst = act2.at[pl.ds(pl.multiple_of(b * sub, sub), sub)]
         return remote(src, dst, gss.at[3 + b], grs.at[3 + b], core)
 
     def asum(b):
         acore(b).wait()
-        got = hid[pl.ds(pl.multiple_of(b * sub, sub), sub), :]
+        got = act2[pl.ds(pl.multiple_of(b * sub, sub), sub), :]
         rows = pl.ds(pl.multiple_of(b * sub, sub), sub)
         agrad[rows, :] = (agrad[rows, :].astype(f32) + got.astype(f32)).astype(bf16)
 
     def astart(b, theirs, ours):
-        hid[pl.ds(pl.multiple_of((4 + b) * sub, sub), sub), :] = theirs.astype(bf16)
+        act2[pl.ds(pl.multiple_of((4 + b) * sub, sub), sub), :] = theirs.astype(bf16)
         acore(b).start()
         agrad[pl.ds(pl.multiple_of(b * sub, sub), sub), :] = ours.astype(bf16)
 
@@ -528,9 +566,9 @@
 
     def tree(b, phase):
         mine = agrad.at[pl.ds(pl.multiple_of(b * sub + y * hs, hs), hs)]
-        final = hid.at[pl.ds(pl.multiple_of(b * sub + y * hs, hs), hs)]
-        buf_a = x1b.at[pl.ds(b * sub, hs)]
-        buf_b = x1b.at[pl.ds(b * sub + hs, hs)]
+        final = act2.at[pl.ds(pl.multiple_of(b * sub + y * hs, hs), hs)]
+        buf_a = x1b.at[pl.ds(pl.multiple_of(b * sub, hs), hs)]
+        buf_b = x1b.at[pl.ds(pl.multiple_of(b * sub + hs, hs), hs)]
         buf_c = dmb.at[b, 0, pl.ds(0, hs)]
         c0 = lambda: remote(agrad.at[pl.ds(pl.multiple_of(b * sub + (1 - y) * hs, hs), hs)], buf_a, fas.at[b, 0], far.at[b, 0], ydev)
         c1 = lambda: remote(mine, buf_b, fas.at[b, 1], far.at[b, 1], zdev)
@@ -627,59 +665,6 @@
         second = both[:, 1].reshape(sub, width)
         astart(0, jnp.where(c == 0, second, first), jnp.where(c == 0, first, second))
 
-    def at_step(q, n):
-        return when(q == n)
-
-    def back(q, carry):
-        j, i = q // NCH, q % NCH
-        attend_back(j, i)
-
-        @at_step(q, 0)
-        def _():
-            mlp_grads()
-
-        @when(i == NCH - 1)
-        def _():
-            @when(j < hc - 1)
-            def _():
-                kv_send(j)
-
-        @when(jnp.logical_and(i == 0, j > 0))
-        def _():
-            kv_finish(j - 1)
-            qkv_grads(j - 1)
-
-        @at_step(q, 3)
-        def _():
-            out_grads()
-
-        @at_step(q, 4)
-        def _():
-            asum(0)
-
-        @when(jnp.logical_and(i == 1, j > 0))
-        def _():
-            asum(j)
-
-        for n in range(len(doubling) + 1):
-
-            @at_step(q, min(2 + n, NCH * hc - 1))
-            def _():
-                gain_step(n)
-
-        if ring:
-            for b, ph, n in TREE_PLAN:
-
-                @at_step(q, n)
-                def _():
-                    tree(b, ph)
-
-            for extra in range(2):
-                ring_step(2 * q + extra)
-        return carry
-
-    lax.fori_loop(0, NCH * hc, back, 0)
-
     def fcopy(i):
         return remote(snd1.at[i], mrecv.at[i], fss.at[i], frs.at[i], xp)
 
@@ -687,73 +672,132 @@
         cols = pl.ds(pl.multiple_of(i * tq + who * cl, cl), cl)
         d = None
         for cc in range(2):
-            part = dot(dpt[cc, :, cols], wqt[cc], 0, 0)
+            part = dot(dpt[cc, :, cols], wqt[cc].reshape(3 * qw, width), 0, 0)
             d = part if d is None else d + part
         return d
 
-    def rings(first, last):
-        if ring:
-
-            def one(m, carry):
-                ring_step(m)
-                return carry
-
-            lax.fori_loop(first, last, one, 0)
-
-    def trees(*steps):
-        if ring:
-            for b, ph in steps:
-                tree(b, ph)
-
-    last = hc - 1
-    done = 2 * NCH * hc
-    kv_send(last)
-    trees((2, 2), (0, 5), (1, 4))
-    rings(done, done + 2)
-    kv_finish(last)
-    for i in range(NCH):
+    def input_send(i):
         mcopy(i).wait_send()
         snd1[i] = input_terms(i, ox).astype(bf16)
         fcopy(i).start()
-    qkv_grads(last)
-    rings(done + 2, done + 4)
-    asum(1 + last)
-    trees((3, 0), (2, 3), (1, 5))
-    rings(done + 4, done + 7)
-    trees((3, 1), (2, 4))
-    rings(done + 7, done + 10)
-    trees((3, 2), (2, 5))
-    rings(done + 10, done + 13)
-    trees((3, 3))
-    rings(done + 13, done + 16)
-    trees((3, 4))
-
-    for i in range(NCH):
+
+    def dxcopy(i):
+        return pltpu.make_async_copy(ybuf.at[i], out_dx.at[own_of(i)], lsem.at[i])
+
+    def input_finish(i):
         d = input_terms(i, x)
         fcopy(i).wait_recv()
-        own = pl.ds(i * cl, cl)
-        d = rown[own, :] + (d + mrecv[i].astype(f32))
+        d = rown[own_of(i), :] + (d + mrecv[i].astype(f32))
         ycopy(i).wait()
         ybuf[i] = d.astype(bf16)
-        pltpu.make_async_copy(ybuf.at[i], out_dx.at[own], lsem.at[i]).start()
-    rings(done + 16, 3 * (hops + 1))
-    trees((3, 5))
+        dxcopy(i).start()
+
+    def kv_done(j):
+        kv_finish(j)
+        qkv_grads(j)
+
+    handlers = {
+        "S0": attend,
+        "S1": mlp_fwd,
+        "S2": norm_two,
+        "S3": mlp_bwd,
+        "D": lambda i: dcopy(i).start(),
+        "S4": norm_one,
+        "S5": lambda q: attend_back(q // NCH, q % NCH),
+        "kvs": kv_send,
+        "kvf": kv_done,
+        "og": lambda i: out_grads(),
+        "as": asum,
+        "C0": lambda i: weights_free(),
+        "C1": lambda i: buffers_free(),
+        "I": input_send,
+        "F": input_finish,
+    }
+    for n in range(3):
+        handlers["G%d" % n] = functools.partial(lambda n, i: grad(n), n)
+        handlers["gs%d" % n] = functools.partial(lambda n, i: gsum(n), n)
+    for n in range(len(doubling) + 1):
+        handlers["N%d" % n] = functools.partial(lambda n, i: gain_step(n), n)
+    if ring:
+        for ph in range(6):
+            handlers["T%d" % ph] = functools.partial(lambda ph, b: tree(b, ph), ph)
+
+    plan = [(kind, arg) for kind, arg in make_plan(len(doubling)) if kind in handlers or kind == "R"]
+    big = []
+    count = 0
+    for kind, arg in plan:
+        if kind == "R":
+            count += arg
+            big[-1][2] = count
+        else:
+            big.append([kind, arg, count])
+
+    total_ring = 3 * (hops + 1 + 2 * RING_LAG)
+    big[-1][2] = total_ring
+    kinds = sorted({b[0] for b in big}, key=[b[0] for b in big].index)
+
+    packed = [
+        kinds.index(kind) + 64 * (arg + 16 * min(ends, total_ring)) for kind, arg, ends in big
+    ]
+
+    def entry(t):
+        value = packed[0]
+        for n in range(1, len(packed)):
+            value = jnp.where(t >= n, packed[n], value)
+        return value % 64, (value // 64) % 16, value // 1024
+
+    def dispatch(code, arg, first, last):
+        if last - first == 1:
+            handlers[kinds[first]](arg)
+            return
+        middle = (first + last) // 2
+
+        @when(code < middle)
+        def _():
+            dispatch(code, arg, first, middle)
+
+        @when(code >= middle)
+        def _():
+            dispatch(code, arg, middle, last)
+
+    def one_step(t, done):
+        code, arg, ends = entry(t)
+        dispatch(code, arg, 0, len(kinds))
+        if not ring:
+            return done
+
+        def ring_one(m, carry):
+            ring_step(m)
+            return carry
+
+        lax.fori_loop(done, ends, ring_one, 0)
+        return ends
+
+    lax.fori_loop(0, len(big), one_step, 0)
 
     def result_copies():
-        return [
-            pltpu.make_async_copy(wm.at[pl.ds(3 if ring else 0, 3)], g_mlp, gls.at[0]),
-            pltpu.make_async_copy(
-                hid.at[pl.ds(0, (1 + hc) * sub)] if ring else agrad, g_att, gls.at[1]
-            ),
+        first, third = (3, 7) if ring else (0, 6)
+        att = act2 if ring else agrad
+        cps = [
+            pltpu.make_async_copy(wm.at[pl.ds(first, 2)], g_mlp.at[pl.ds(0, 2)], gls.at[0]),
+            pltpu.make_async_copy(wm.at[third], g_mlp.at[2], gls.at[1]),
+            pltpu.make_async_copy(att.at[pl.ds(0, sub)], g_out, gls.at[2]),
         ]
+        for j in range(hc):
+            for n in range(3):
+                rows = pl.ds((1 + j) * sub + n * HEAD, HEAD)
+                cps.append(
+                    pltpu.make_async_copy(att.at[rows], g_qkv.at[n, j], gls.at[len(cps)])
+                )
+        return cps
 
     for cp in result_copies():
         cp.start()
-    g_gain[...] = gbuf[...]
+    g_ga[...] = gbuf[0:1, :]
+    g_gm[...] = gbuf[1:2, :]
 
     for i in range(NCH):
-        own = pl.ds(i * cl, cl)
-        pltpu.make_async_copy(ybuf.at[i], out_dx.at[own], lsem.at[i]).wait()
+        dxcopy(i).wait()
         xcopy(i).wait_send()
         for cp in kvcopies(i):
             cp.wait_send()
@@ -761,7 +805,7 @@
         dcopy(i).wait_send()
         acopy(i).wait_send()
         fcopy(i).wait_send()
-    for w in (w_q, w_o, w_ox, w_oxc, w_g, w_u, w_d):
+    for w in (*w_q, w_o, w_ox, w_oxc, w_g, w_u, w_d):
         w.wait_send()
     if ring:
         for u in range(3):
@@ -771,11 +815,28 @@
         cp.wait()
 
 
-TREE_PLAN = (
-    (0, 0, 4), (0, 1, 6), (0, 2, 8), (0, 3, 10), (0, 4, 11),
-    (1, 0, 5), (1, 1, 7), (1, 2, 9), (1, 3, 11),
-    (2, 0, 9), (2, 1, 11),
-)
+RING_LAG = 2
+
+
+def make_plan(doublings):
+    plan = [
+        ("S0", 0), ("S0", 1), ("S0", 2), ("S0", 3), ("S1", 0), ("S1", 1), ("S1", 2), ("S2", 0),
+        ("S1", 3), ("S2", 1), ("S2", 2), ("S3", 0), ("S2", 3), ("D", 0), ("S3", 1), ("D", 1),
+        ("S3", 2), ("D", 2), ("S3", 3), ("C0", 0), ("D", 3), ("G2", 0), ("S4", 0), ("G0", 0),
+        ("gs2", 0), ("R", 3), ("S4", 1), ("S4", 2), ("G1", 0), ("R", 3), ("gs0", 0), ("S4", 3),
+        ("S5", 0), ("N0", 0), ("R", 3), ("gs1", 0), ("C1", 0), ("S5", 4), ("N1", 0), ("R", 1),
+        ("S5", 1), ("N2", 0), ("R", 3), ("S5", 2), ("N3", 0), ("R", 2), ("S5", 3), ("N4", 0),
+        ("R", 2), ("og", 0), ("R", 1), ("kvs", 0), ("S5", 5), ("N5", 0), ("R", 2), ("kvf", 0),
+        ("R", 1), ("as", 0), ("T0", 0), ("S5", 6), ("R", 3), ("as", 1), ("T0", 1), ("S5", 7),
+        ("T1", 0), ("kvs", 1), ("S5", 8), ("R", 3), ("kvf", 1), ("T2", 0), ("S5", 9), ("T1", 1),
+        ("R", 1), ("as", 2), ("T0", 2), ("S5", 10), ("T3", 0), ("R", 2), ("T2", 1), ("S5", 11),
+        ("T1", 2), ("R", 1), ("kvs", 2), ("T4", 0), ("R", 2), ("kvf", 2), ("T3", 1), ("T2", 2),
+        ("I", 0), ("I", 1), ("I", 2), ("R", 1), ("as", 3), ("T0", 3), ("T5", 0), ("I", 3),
+        ("R", 2), ("T4", 1), ("F", 0), ("T3", 2), ("R", 1), ("T1", 3), ("R", 2), ("T4", 2),
+        ("T5", 1), ("R", 1), ("T2", 3), ("R", 2), ("F", 1), ("F", 2), ("F", 3), ("T3", 3),
+        ("T5", 2), ("R", 1), ("T4", 3), ("R", 3), ("T5", 3), ("R", 11),
+    ]
+    return plan + [("N%d" % n, 0) for n in range(6, doublings + 1)]
 
 
 def on_device(
@@ -790,27 +851,15 @@
     tq = 2 * cl
     ntok = 2 * length
     nkey = 2 * ntok
-    h = lax.axis_index("heads")
-    c = h % 2
-
-    order = jnp.arange(nkey, dtype=jnp.int32).reshape(2, NCH, 2, cl)
-    cores = lax.broadcasted_iota(jnp.int32, order.shape, 0)
-    chunk = lax.broadcasted_iota(jnp.int32, order.shape, 1)
-    xs = lax.broadcasted_iota(jnp.int32, order.shape, 2)
-    place = lax.broadcasted_iota(jnp.int32, order.shape, 3)
-    position = (2 * xs + cores) * length + chunk * cl + place
-    valid = position.reshape(1, nkey) < lengths[0]
-    row = lax.broadcasted_iota(jnp.int32, (HEAD, nkey), 0)
-    augk = jnp.where(
-        row == 0, jnp.where(valid, 0.0, -1e30), jnp.where(row < 4, 1.0, 0.0)
-    ).astype(bf16)
-    here = ((2 * xs[0] + c) * length + chunk[0] * cl + place[0]).reshape(1, ntok).astype(f32)
+    cores, chunk, xs, place = np.meshgrid(
+        np.arange(2), np.arange(NCH), np.arange(2), np.arange(cl), indexing="ij"
+    )
+    position = ((2 * xs + cores) * length + chunk * cl + place).reshape(2, ntok)
     half = HEAD // 2
-    freqs = rope_base ** (-jnp.arange(half).astype(f32) / half)
-    angles = freqs[:, None] * here
-    cos_t, sin_t = jnp.cos(angles), jnp.sin(angles)
-
-    wqt = w_qkv.reshape(3, width, hc, HEAD).transpose(2, 0, 3, 1).reshape(3 * qw, width)
+    freqs = rope_base ** (-np.arange(half) / half)
+    angles = freqs[None, :, None] * position[:, None, :]
+    turns = np.stack([np.cos(angles), np.sin(angles)], axis=1).astype(np.float32)
+    places = position.reshape(1, nkey).astype(np.int32)
 
     hbm = pl.BlockSpec(memory_space=pl.ANY)
     vmem = pl.BlockSpec(memory_space=pltpu.VMEM)
@@ -821,9 +870,9 @@
     scratch = [
         V((NCH, 2, cl, width), bf16),
         V((length, width), bf16),
-        V((2, 3 * qw, width), bf16),
+        V((2, hc, 3, HEAD, width), bf16),
         V((2, hc, 2, HEAD, width), bf16),
-        V((6, width, fq), bf16),
+        V((9, width, fq), bf16),
         V((hc, 2, 2 * HEAD, nkey), bf16),
         V((hc, 2, 2 * HEAD, nkey), bf16),
         V((2, hc, ntok, 2 * HEAD), bf16),
@@ -843,18 +892,17 @@
         V((NCH, cl, width), bf16),
         V((NCH, cl, width), bf16),
         V((2, cl, width), f32),
-        V((2, cl, width), f32),
-        V((2, cl, width), f32),
         V((2, cl, 128), f32),
         V((2, 2, 2 * HEAD, nkey), f32),
         V((hc, 2, 2 * HEAD, ntok), bf16),
         V((2, 3 * qw, ntok), bf16),
         V((NCH, cl, width), bf16),
-        V((width, fq), bf16),
         V(((1 + hc) * 3 * HEAD, width), bf16),
         V((8, width), f32),
         V((doublings, 8, width), f32),
-        dma((NCH + 6,)),
+        V((2, HEAD // 2, ntok), f32),
+        dma((NCH + 9,)),
+        dma((3,)), dma((3,)),
         dma((7,)), dma((7,)),
         dma((NCH,)), dma((NCH,)),
         dma((NCH, 4)), dma((NCH, 4)),
@@ -865,37 +913,38 @@
         dma((NCH,)), dma((NCH,)),
         dma((hc,)), dma((hc,)),
         dma((NCH,)), dma((NCH,)),
-        dma((4 + hc,)), dma((4 + hc,)), dma((2,)),
+        dma((4 + hc,)), dma((4 + hc,)), dma((3 + 3 * hc,)),
         dma((3, 2, 14)), dma((3, 2, 14)),
         dma((1 + hc, 5)), dma((1 + hc, 5)),
         dma((doublings,)), dma((doublings,)),
         dma((NCH,)),
-        pltpu.SemaphoreType.REGULAR((3,)),
+        pltpu.SemaphoreType.REGULAR((4,)),
     ]
     outs = pl.pallas_call(
         functools.partial(layer_kernel, nrows),
         out_shape=[
             S((length, width), bf16), S((length, width), bf16),
-            S((3, width, fq), bf16), S(((1 + hc) * 3 * HEAD, width), bf16), S((8, width), f32),
+            S((3, width, fq), bf16), S((qw, width), bf16), S((3, hc, HEAD, width), bf16),
+            S((1, width), f32), S((1, width), f32),
         ],
-        in_specs=[hbm] * 7 + [vmem] * 5,
-        out_specs=[hbm] * 4 + [vmem],
+        in_specs=[hbm] * 8 + [pl.BlockSpec(memory_space=pltpu.SMEM)] + [vmem] * 3,
+        out_specs=[hbm] * 5 + [vmem] * 2,
         scratch_shapes=scratch,
         compiler_params=pltpu.CompilerParams(
             collective_id=0, has_side_effects=True, vmem_limit_bytes=VLIM
         ),
     )(
-        tokens[0], cotangent[0], wqt, w_out.reshape(hc, HEAD, width), w_gate, w_up, w_down,
-        gain_attn[None], gain_mlp[None], cos_t, sin_t, augk,
+        tokens[0], cotangent[0],
+        w_qkv.transpose(0, 2, 1).reshape(3, hc, HEAD, width), w_out.reshape(hc, HEAD, width), w_gate, w_up, w_down,
+        jnp.asarray(turns), lengths, gain_attn, gain_mlp, jnp.asarray(places),
     )
-    y, dx, g_mlp, g_att, g_gain = outs
+    y, dx, g_mlp, g_out, g_qkv, g_ga, g_gm = outs
     if nrows != 8:
-        g_mlp, g_att = lax.psum((g_mlp, g_att), "rows")
-    g_att = g_att.reshape(1 + hc, 3 * HEAD, width)
-    grad_qkv = g_att[1:].reshape(hc, 3, HEAD, width).transpose(1, 3, 0, 2)
+        g_mlp, g_out, g_qkv = lax.psum((g_mlp, g_out, g_qkv), "rows")
     return (
-        y[None], dx[None], grad_qkv.astype(f32).reshape(3, width, qw), g_att[0].astype(f32),
-        g_mlp[0].astype(f32), g_mlp[1].astype(f32), g_mlp[2].astype(f32), g_gain[0], g_gain[1],
+        y[None], dx[None], g_qkv.astype(f32).reshape(3, qw, width).transpose(0, 2, 1),
+        g_out.astype(f32), g_mlp[0].astype(f32), g_mlp[1].astype(f32), g_mlp[2].astype(f32),
+        g_ga[0], g_gm[0],
     )
 
 

time: 255 us -> 235 us (0.922)
  Pallas kernels: 237 us -> 223 us
  local copies, waits for them, and re-layouts: 7.89 us -> 1.78 us
    pallas_call x1, Pallas kernels: 237 us -> 223 us  [on_device(): pl.pallas_call(functools.partial(layer_kernel, nrows), out_shape=[S((leng...]
    reshape x2 -> x0, local copies, waits for them, and re-layouts: 3.46 us -> none  [the longest x1 2.13 us: on_device(): w_qkv.reshape(3, width, hc, HEAD).transpose(2, 0, 3, 1)]
where the time goes in v3:
time: 235 us
  Pallas kernels  223 us (95%)
  other arithmetic  8.66 us (4%)
    pallas_call x1, Pallas kernels, on_device(): pl.pallas_call(functools.partial(layer_kernel, nrows), out_shape=[S((leng...  223 us
    convert_element_type x1, other arithmetic, on_device(): g_mlp[2].astype(f32)  5.19 us

profile of v3, /device:TPU:0, one launch (start us, length us, event | category | flops | bytes accessed | tf_op | source)
XLA Modules:
  0.0 234.8 jit_solution(2759549462017047706)
XLA Ops:
  1.3 223.0 %shard_map.187 = (bf16[512,768]{1,0:T(8,128)(2,1)}, bf16[512,768]{1,0:T(8,128)(2,1)}, bf16[3,768,768]{2,1,0:T(8,128)(2,1)}, bf16[192,768]{1,0:T(8,128)(2,1)}, bf...) custom-call(bf16[512,768]{1,0:T(8,128)(2,1)} %bitcast.25, bf16[512,768]{1,0:T(8,128)(2,1)} %bitcast.26, ...), custom_call_target="tpu_custom_call" | custom-call | tf_op jit(solution)/shard_map/pallas_call | solution.py:923
  224.3 0.0 copy-start
  224.3 5.2 %bitcast_convert_fusion = (f32[768,768]{1,0:T(8,128)}, f32[768,768]{1,0:T(8,128)}, f32[768,768]{1,0:T(8,128)}) fusion(bf16[3,768,768]{2,1,0:T(8,128)(2,1)} %get-tuple-element.20), kind=kLoop, calls=%fused_computation.1 | loop fusion | flops 1769472 | bytes 10616832 | tf_op jit(solution)/shard_map/convert_element_type | solution.py:946
  229.5 0.0 copy-start.3
  229.5 0.0 copy-start.5
  229.5 0.0 copy-start.4
  229.5 0.0 copy-start.2
  229.5 0.0 copy-done
  229.5 0.0 copy-start.1
  229.5 1.4 convert_bitcast_fusion
  230.9 0.0 copy-done.3
  230.9 0.9 convert_element_type.22
  231.8 0.0 copy-done.5
  231.8 0.6 reduce
  232.4 0.0 copy-done.4
  232.4 0.6 reduce.1
  233.0 0.0 copy-done.2
  233.0 0.9 copy.24
  233.9 0.0 copy-done.1
  233.9 0.9 copy.25
Async XLA Ops:
  224.3 5.2 %copy-start = (bf16[3,3,64,768]{3,2,1,0:T(8,128)(2,1)S(1)}, bf16[3,3,64,768]{3,2,1,0:T(8,128)(2,1)}, u32[]{:S(2)}) copy-start(bf16[3,3,64,768]{3,2,1,0:T(8,128)(2,1)} %get-tuple-element.18) | copy-start | bytes 2654212
  229.5 1.4 copy-start.3
  229.5 2.3 copy-start.5
  229.5 2.9 %copy-start.4 = (f32[1,768]{1,0:T(1,128)S(1)}, f32[1,768]{1,0:T(1,128)}, u32[]{:S(2)}) copy-start(f32[1,768]{1,0:T(1,128)} %get-tuple-element.22) | copy-start | bytes 9220
  229.5 3.5 %copy-start.2 = (bf16[512,768]{1,0:T(8,128)(2,1)S(1)}, bf16[512,768]{1,0:T(8,128)(2,1)}, u32[]{:S(2)}) copy-start(bf16[512,768]{1,0:T(8,128)(2,1)} %get-tuple-element.16) | copy-start | bytes 2359300
  229.5 4.4 %copy-start.1 = (bf16[512,768]{1,0:T(8,128)(2,1)S(1)}, bf16[512,768]{1,0:T(8,128)(2,1)}, u32[]{:S(2)}) copy-start(bf16[512,768]{1,0:T(8,128)(2,1)} %get-tuple-element.17) | copy-start | bytes 2359300

commit v4 on v3

--- a/solution.py
+++ b/solution.py
@@ -815,7 +815,7 @@
         cp.wait()
 
 
-RING_LAG = 2
+RING_LAG = 1
 
 
 def make_plan(doublings):
@@ -823,20 +823,93 @@
         ("S0", 0), ("S0", 1), ("S0", 2), ("S0", 3), ("S1", 0), ("S1", 1), ("S1", 2), ("S2", 0),
         ("S1", 3), ("S2", 1), ("S2", 2), ("S3", 0), ("S2", 3), ("D", 0), ("S3", 1), ("D", 1),
         ("S3", 2), ("D", 2), ("S3", 3), ("C0", 0), ("D", 3), ("G2", 0), ("S4", 0), ("G0", 0),
-        ("gs2", 0), ("R", 3), ("S4", 1), ("S4", 2), ("G1", 0), ("R", 3), ("gs0", 0), ("S4", 3),
-        ("S5", 0), ("N0", 0), ("R", 3), ("gs1", 0), ("C1", 0), ("S5", 4), ("N1", 0), ("R", 1),
-        ("S5", 1), ("N2", 0), ("R", 3), ("S5", 2), ("N3", 0), ("R", 2), ("S5", 3), ("N4", 0),
-        ("R", 2), ("og", 0), ("R", 1), ("kvs", 0), ("S5", 5), ("N5", 0), ("R", 2), ("kvf", 0),
-        ("R", 1), ("as", 0), ("T0", 0), ("S5", 6), ("R", 3), ("as", 1), ("T0", 1), ("S5", 7),
-        ("T1", 0), ("kvs", 1), ("S5", 8), ("R", 3), ("kvf", 1), ("T2", 0), ("S5", 9), ("T1", 1),
-        ("R", 1), ("as", 2), ("T0", 2), ("S5", 10), ("T3", 0), ("R", 2), ("T2", 1), ("S5", 11),
-        ("T1", 2), ("R", 1), ("kvs", 2), ("T4", 0), ("R", 2), ("kvf", 2), ("T3", 1), ("T2", 2),
-        ("I", 0), ("I", 1), ("I", 2), ("R", 1), ("as", 3), ("T0", 3), ("T5", 0), ("I", 3),
-        ("R", 2), ("T4", 1), ("F", 0), ("T3", 2), ("R", 1), ("T1", 3), ("R", 2), ("T4", 2),
-        ("T5", 1), ("R", 1), ("T2", 3), ("R", 2), ("F", 1), ("F", 2), ("F", 3), ("T3", 3),
-        ("T5", 2), ("R", 1), ("T4", 3), ("R", 3), ("T5", 3), ("R", 11),
+        ("gs2", 0), ("R", 3), ("S4", 1), ("S4", 2), ("gs0", 0), ("R", 3), ("S4", 3), ("G1", 0),
+        ("R", 2), ("S5", 0), ("N0", 0), ("gs1", 0), ("R", 3), ("C1", 0), ("S5", 1), ("N1", 0),
+        ("R", 2), ("S5", 2), ("N2", 0), ("R", 3), ("S5", 3), ("N3", 0), ("R", 2), ("og", 0),
+        ("R", 1), ("kvs", 0), ("S5", 4), ("N4", 0), ("R", 3), ("kvf", 0), ("as", 0), ("T0", 0),
+        ("S5", 5), ("N5", 0), ("R", 3), ("as", 1), ("T0", 1), ("S5", 6), ("T1", 0), ("S5", 7),
+        ("R", 3), ("kvs", 1), ("T2", 0), ("S5", 8), ("T1", 1), ("R", 1), ("kvf", 1), ("R", 1),
+        ("S5", 9), ("T2", 1), ("T3", 0), ("R", 2), ("as", 2), ("T0", 2), ("S5", 10), ("R", 1),
+        ("S5", 11), ("T1", 2), ("T3", 1), ("T4", 0), ("R", 2), ("kvs", 2), ("R", 1), ("kvf", 2),
+        ("T2", 2), ("T5", 0), ("T4", 1), ("I", 0), ("I", 1), ("I", 2), ("R", 1), ("as", 3),
+        ("T0", 3), ("I", 3), ("R", 2), ("T3", 2), ("F", 0), ("T5", 1), ("R", 1), ("T1", 3),
+        ("T4", 2), ("R", 3), ("F", 1), ("F", 2), ("T5", 2), ("T2", 3), ("R", 2), ("T3", 3),
+        ("R", 1), ("F", 3), ("T4", 3), ("R", 4), ("T5", 3), ("R", 1),
     ]
     return plan + [("N%d" % n, 0) for n in range(6, doublings + 1)]
+
+
+def results_kernel(y, dx, mlp, out, qkv, ga, gm, y2, dx2, gate2, up2, down2, out2, qkv2, ga2, gm2,
+                   low, wide, held, in_sem, out_sem, row_sem):
+    width, qw = mlp.shape[1], out.shape[0]
+    half = width // 2
+    pairs = []
+    for n, dst in enumerate((gate2, up2, down2)):
+        for p in range(2):
+            rows = pl.ds(p * half, half)
+            pairs.append((mlp.at[n, rows], dst.at[rows], half))
+    for n in range(3):
+        pairs.append((qkv.at[n], qkv2.at[n], qw))
+    pairs.append((out, out2, qw))
+    moves = []
+    at = 0
+    for k, (src, dst, size) in enumerate(pairs):
+        part = pl.ds(at, size)
+        moves.append((
+            pltpu.make_async_copy(src, low.at[part], in_sem.at[k]),
+            pltpu.make_async_copy(wide.at[part], dst, out_sem.at[k]),
+            slice(at, at + size),
+        ))
+        at += size
+    rows = [
+        (
+            pltpu.make_async_copy(src, held.at[n], row_sem.at[n]),
+            pltpu.make_async_copy(held.at[n], dst, row_sem.at[2 + n]),
+        )
+        for n, (src, dst) in enumerate(((y, y2), (dx, dx2)))
+    ]
+    for load, _, _ in moves:
+        load.start()
+    for load, _ in rows:
+        load.start()
+    ga2[...] = ga[0]
+    gm2[...] = gm[0]
+    for load, store, part in moves:
+        load.wait()
+        wide[part, :] = low[part, :].astype(f32)
+        store.start()
+    for load, store in rows:
+        load.wait()
+        store.start()
+    for _, store, _ in moves:
+        store.wait()
+    for _, store in rows:
+        store.wait()
+
+
+def results(y, dx, g_mlp, g_out, g_qkv, g_ga, g_gm):
+    _, width, fq = g_mlp.shape
+    qw = g_out.shape[0]
+    total = 3 * width + 4 * qw
+    vmem = pl.BlockSpec(memory_space=pltpu.VMEM)
+    hbm = pl.BlockSpec(memory_space=pl.ANY)
+    S = jax.ShapeDtypeStruct
+    dma = pltpu.SemaphoreType.DMA
+    return pl.pallas_call(
+        results_kernel,
+        out_shape=[
+            S(y.shape, bf16), S(dx.shape, bf16), S((width, fq), f32), S((width, fq), f32),
+            S((fq, width), f32), S((qw, width), f32), S((3, qw, width), f32),
+            S((width,), f32), S((width,), f32),
+        ],
+        in_specs=[hbm] * 5 + [vmem] * 2,
+        out_specs=[hbm] * 7 + [vmem] * 2,
+        scratch_shapes=[
+            pltpu.VMEM((total, width), bf16), pltpu.VMEM((total, width), f32),
+            pltpu.VMEM((2, *y.shape), bf16), dma((10,)), dma((10,)), dma((4,)),
+        ],
+        compiler_params=pltpu.CompilerParams(vmem_limit_bytes=VLIM),
+    )(y, dx, g_mlp, g_out, g_qkv, g_ga, g_gm)
 
 
 def on_device(
@@ -941,10 +1014,11 @@
     y, dx, g_mlp, g_out, g_qkv, g_ga, g_gm = outs
     if nrows != 8:
         g_mlp, g_out, g_qkv = lax.psum((g_mlp, g_out, g_qkv), "rows")
+    y, dx, gate2, up2, down2, out2, qkv2, g_ga, g_gm = results(
+        y, dx, g_mlp, g_out, g_qkv.reshape(3, qw, width), g_ga, g_gm
+    )
     return (
-        y[None], dx[None], g_qkv.astype(f32).reshape(3, qw, width).transpose(0, 2, 1),
-        g_out.astype(f32), g_mlp[0].astype(f32), g_mlp[1].astype(f32), g_mlp[2].astype(f32),
-        g_ga[0], g_gm[0],
+        y[None], dx[None], qkv2.transpose(0, 2, 1), out2, gate2, up2, down2, g_ga, g_gm,
     )
 
 

time: 235 us -> 220 us (0.936)
  other arithmetic: 8.66 us -> 0 us
  Pallas kernels: 223 us -> 218 us
    pallas_call x1, Pallas kernels: 223 us -> 212 us  [on_device(): pl.pallas_call(functools.partial(layer_kernel, nrows), out_shape=[S((leng...]
    pallas_call x0 -> x1, Pallas kernels: none -> 6.96 us  [results(): pl.pallas_call(results_kernel, out_shape=[S(y.shape, bf16), S(dx.shape, b...]
    convert_element_type x2 -> x0, other arithmetic: 6.04 us -> none  [the longest x1 5.19 us: on_device(): g_mlp[2].astype(f32)]
where the time goes in v4:
time: 220 us
  Pallas kernels  218 us (99%)
    pallas_call x1, Pallas kernels, on_device(): pl.pallas_call(functools.partial(layer_kernel, nrows), out_shape=[S((leng...  212 us
    pallas_call x1, Pallas kernels, results(): pl.pallas_call(results_kernel, out_shape=[S(y.shape, bf16), S(dx.shape, b...  6.96 us

profile of v4, /device:TPU:0, one launch (start us, length us, event | category | flops | bytes accessed | tf_op | source)
XLA Modules:
  0.0 219.8 jit_solution(6223482536306624334)
XLA Ops:
  1.3 211.5 %shard_map.187 = (bf16[512,768]{1,0:T(8,128)(2,1)}, bf16[512,768]{1,0:T(8,128)(2,1)}, bf16[3,768,768]{2,1,0:T(8,128)(2,1)}, bf16[192,768]{1,0:T(8,128)(2,1)}, bf...) custom-call(bf16[512,768]{1,0:T(8,128)(2,1)} %bitcast.12, bf16[512,768]{1,0:T(8,128)(2,1)} %bitcast.13, ...), custom_call_target="tpu_custom_call" | custom-call | tf_op jit(solution)/shard_map/pallas_call | solution.py:996
  212.8 7.0 %shard_map.188 = (bf16[512,768]{1,0:T(8,128)(2,1)}, bf16[512,768]{1,0:T(8,128)(2,1)}, f32[768,768]{1,0:T(8,128)}, f32[768,768]{1,0:T(8,128)}, f32[768,768]{1,0:T...) custom-call(bf16[512,768]{1,0:T(8,128)(2,1)} %get-tuple-element.25.y, ...), custom_call_target="tpu_custom_call" | custom-call | tf_op jit(solution)/shard_map/pallas_call | solution.py:898

commit v5 on v4

--- a/solution.py
+++ b/solution.py
@@ -349,7 +349,7 @@
         dab[i, x] = dr.astype(bf16)
         acopy(i).start()
 
-    kb = min(1024, nkey)
+    kb = min(2048, nkey)
 
     def attend_back(j, i):
         rows = rows_of(i)

time: 220 us -> 220 us (level)
  no operation moved by 1% of the time
where the time goes in v5:
time: 220 us
  Pallas kernels  219 us (100%)
    pallas_call x1, Pallas kernels, on_device(): pl.pallas_call(functools.partial(layer_kernel, nrows), out_shape=[S((leng...  212 us
    pallas_call x1, Pallas kernels, results(): pl.pallas_call(results_kernel, out_shape=[S(y.shape, bf16), S(dx.shape, b...  6.96 us

profile of v5, /device:TPU:0, one launch (start us, length us, event | category | flops | bytes accessed | tf_op | source)
XLA Modules:
  0.0 219.8 jit_solution(652821603454503917)
XLA Ops:
  1.3 211.6 %shard_map.187 = (bf16[512,768]{1,0:T(8,128)(2,1)}, bf16[512,768]{1,0:T(8,128)(2,1)}, bf16[3,768,768]{2,1,0:T(8,128)(2,1)}, bf16[192,768]{1,0:T(8,128)(2,1)}, bf...) custom-call(bf16[512,768]{1,0:T(8,128)(2,1)} %bitcast.12, bf16[512,768]{1,0:T(8,128)(2,1)} %bitcast.13, ...), custom_call_target="tpu_custom_call" | custom-call | tf_op jit(solution)/shard_map/pallas_call | solution.py:996
  212.9 7.0 %shard_map.188 = (bf16[512,768]{1,0:T(8,128)(2,1)}, bf16[512,768]{1,0:T(8,128)(2,1)}, f32[768,768]{1,0:T(8,128)}, f32[768,768]{1,0:T(8,128)}, f32[768,768]{1,0:T...) custom-call(bf16[512,768]{1,0:T(8,128)(2,1)} %get-tuple-element.25.y, ...), custom_call_target="tpu_custom_call" | custom-call | tf_op jit(solution)/shard_map/pallas_call | solution.py:898
